TPU v7x, 32 devices: a whole 2x2x4 slice. The times are simulated.
32 devices in a mesh: grp: 2 (over y), pair: 4 (over z), rng: 4 (over x, core).
Axes of the slice: x: 2, y: 2, z: 4, core: 2. Of those that a mesh axis runs over, the one named last changes fastest.
Arguments:
- integrals: bfloat16 [12288, 16384], P(('grp', 'pair'), 'rng'), parts along dimension 0, may hold values from -0.046875 to 0.046875
- coefficients: bfloat16 [8192, 16], P('grp'), parts along dimension 0, may hold values from -6 to 6
- ket_shells: int32 [512, 2], P(('grp', 'rng')), parts along dimension 0, may hold values from 0 to 511
- block_ids: int32 [192], P(('grp', 'pair')), parts along dimension 0, may hold values from -1 to 47, as said below
- pair_owner: int32 [256], replicated, may hold values from 0 to 255, each once
Outputs:
- half: float32 [512, 3072], P(('grp', 'pair', 'rng')), parts along dimension 0
There are 2 independent parts, one for each index of `grp`. A program takes and returns all parts, laid end to end along the dimension named above; an argument that names none is the same for every part. Nothing has to cross between parts.
Inputs may be any that keep to these rules, and one draw needn't show every extreme that they name: `block_ids`: -1 marks an empty slot; each block 0 to 47 stands in exactly one slot; of the 24 slots of one index of pair, 24, 12 or 6 are filled (a quarter, a quarter and half of the indices in every aligned group of four, in an order drawn), at positions drawn.
All inputs are finite; a program needn't handle non-finite values.
Results may differ from a plain program's by a relative error of at most 0.0029.
Values sent between devices are 32-bit elements; how exact they have to be, the bound alone decides.
No kernel may reach another device: no remote copies, remote signals or barrier semaphores. Data moves between devices by JAX's collectives and lax.ppermute only.
A program may use at most 128 MiB of HBM per device.

v0:
```python
import jax
import jax.numpy as jnp
from jax import lax
from jax.sharding import PartitionSpec as P

SHELL = 8
BLOCK_PAIRS = 64
NIJ = 256


def local(integrals, coefficients, ket_shells, block_ids, pair_owner):
    offsets = jnp.arange(SHELL, dtype=jnp.int32)
    coef_full = coefficients.astype(jnp.float32)
    lam_coef = coef_full[ket_shells[:, 0:1] * SHELL + offsets[None, :]]
    sig_coef = coef_full[ket_shells[:, 1:2] * SHELL + offsets[None, :]]
    pair_cols = jnp.einsum("kli,ksj->ijkls", lam_coef, sig_coef).reshape(NIJ, integrals.shape[1])
    pair_cols = pair_cols[pair_owner].astype(jnp.bfloat16)
    partial_value = lax.dot_general(
        pair_cols, integrals, (((1,), (1,)), ((), ())), preferred_element_type=jnp.float32
    )
    moved_rows = lax.all_to_all(partial_value, "pair", split_axis=0, concat_axis=1, tiled=True)
    owned_rows = lax.psum_scatter(moved_rows, "rng", scatter_dimension=0, tiled=True)
    all_ids = lax.all_gather(block_ids, "pair", axis=0, tiled=True)
    slot_total = all_ids.shape[0]
    block_total = slot_total // 2
    targets = jnp.arange(block_total, dtype=jnp.int32)
    slot_numbers = jnp.arange(slot_total, dtype=jnp.int32)
    source = jnp.sum(
        jnp.where(all_ids[None, :] == targets[:, None], slot_numbers[None, :], 0), axis=1
    )
    row_count = owned_rows.shape[0]
    placed = owned_rows.reshape(row_count, slot_total, BLOCK_PAIRS)[:, source, :]
    return placed.reshape(row_count, block_total * BLOCK_PAIRS)


def solution(mesh):
    placed = (
        P(("grp", "pair"), "rng"),
        P("grp", None),
        P(("grp", "rng"), None),
        P(("grp", "pair")),
        P(),
    )
    return jax.shard_map(
        local,
        mesh=mesh,
        in_specs=placed,
        out_specs=P(("grp", "pair", "rng"), None),
        check_vma=False,
    )
```

profile of v0, /device:TPU:0, one launch (start us, length us, event | category | flops | bytes accessed | tf_op | source)
XLA Modules:
  0.0 133.8 jit_solution(7348120272431357359)
XLA Ops:
  6.5 0.0 reduce-scatter.2.cloned.1.call-start
  6.5 0.8 multiply_bitcast_fusion.2
  7.3 0.1 compare_select_fusion
  7.4 0.1 reshape.115
  7.5 1.4 %copy.27 = bf16[4096,16]{1,0:T(8,128)(2,1)S(1)} copy(bf16[4096,16]{0,1:T(8,128)(2,1)} %param.6) | data formatting | bytes 262144 | tf_op args[1]
  8.9 1.3 %gather_fusion = bf16[512,16]{1,0:T(8,128)(2,1)S(1)} fusion(bf16[4096,16]{1,0:T(8,128)(2,1)S(1)} %copy.27, s32[1024]{0:T(1024)S(1)} %pad_clamp_fusion.3), kind=kCustom, calls=%fused_computation | custom fusion | bytes 34816 | tf_op jit(solution)/shard_map/gather | solution.py:15
  10.3 0.1 reshape.123
  10.4 1.3 %gather_fusion.1 = bf16[512,16]{1,0:T(8,128)(2,1)S(1)} fusion(bf16[4096,16]{1,0:T(8,128)(2,1)S(1)} %copy.27, s32[1024]{0:T(1024)S(1)} %pad_clamp_fusion.2), kind=kCustom, calls=%fused_computation.1 | custom fusion | bytes 34816 | tf_op jit(solution)/shard_map/gather | solution.py:14
  11.7 6.2 %multiply_bitcast_fusion = bf16[16,16,64,8,8]{1,0,4,3,2:T(8,128)(2,1)} fusion(f32[64,8,16]{2,1,0:T(8,128)S(1)} %bitcast_convert_fusion, f32[64,8,16]{2,1,0:T(8,128)S(1)} %bitcast_convert_fusion.1), kind=kLoop, calls=%fused_computation.4 | loop fusion | flops 2097152 | bytes 2162688 | tf_op jit(solution)/shard_map/kli,ksj->ijkls/transpose | solution.py:16
  18.0 20.5 %reshape.110 = bf16[256,4096]{0,1:T(8,128)(2,1)} reshape(bf16[16,16,64,8,8]{1,0,4,3,2:T(8,128)(2,1)} %multiply_bitcast_fusion) | data formatting | bytes 4194304 | tf_op jit(solution)/shard_map/reshape | solution.py:16
  38.5 0.0 copy-start
  38.5 2.9 %copy.29 = bf16[256,4096]{1,0:T(8,128)(2,1)S(1)} copy(bf16[256,4096]{0,1:T(8,128)(2,1)} %reshape.110) | data formatting | bytes 4194304 | tf_op jit(solution)/shard_map/reshape | solution.py:16
  41.5 0.0 copy-done
  41.5 3.2 %gather_fusion.2 = bf16[256,4096]{1,0:T(8,128)(2,1)} fusion(bf16[256,4096]{1,0:T(8,128)(2,1)S(1)} %copy.29, s32[1024]{0:T(1024)S(1)} %pad_clamp_fusion.1), kind=kCustom, calls=%fused_computation.2 | custom fusion | bytes 4195328 | tf_op jit(solution)/shard_map/gather | solution.py:17
  44.7 7.1 %fusion.3 = f32[256,1536]{1,0:T(8,128)S(1)} fusion(bf16[256,4096]{1,0:T(8,128)(2,1)} %gather_fusion.2, bf16[1536,4096]{1,0:T(8,128)(2,1)} %param.5), kind=kOutput, calls=%fused_computation.22 | convolution fusion | flops 3221225472 | bytes 16252928 | tf_op jit(solution)/shard_map/dot_general | solution.py:18
  51.8 43.1 %all_to_all.19 = f32[4,64,1536]{2,1,0:T(8,128)S(1)} all-to-all(f32[4,64,1536]{2,1,0:T(8,128)S(1)} %bitcast.34), channel_id=1, replica_groups=mesh['grp'=2,'pair'=4,'rng'=4] {'pair'}, dimensions={0} | all-to-all | bytes 3145728 | tf_op jit(solution)/shard_map/all_to_all | solution.py:21
  94.9 0.0 copy-start.2
  94.9 0.0 copy-start.1
  94.9 1.3 copy.33
  96.2 0.0 reduce-scatter.2.cloned.1.call-update
  96.2 0.0 copy-done.2
  96.2 0.6 dynamic-slice
  97.5 0.0 copy-done.1
  97.5 0.2 dynamic-update-slice
  97.7 6.1 %all-reduce = s32[96]{0:T(128)S(1)} all-reduce(s32[96]{0:T(128)S(1)} %dynamic-update-slice), channel_id=1, replica_groups=mesh['grp'=2,'pair'=4,'rng'=4] {'pair'}, use_global_device_ids=true, to_apply=%add | all-reduce | flops 96 | bytes 768
  103.8 0.1 select_reduce_fusion
  103.9 19.7 %reduce-scatter.2.cloned.1.call-done = f32[16,6144]{1,0:T(8,128)} async-done(((f32[64,6144]{1,0:T(8,128)}), f32[16,6144]{1,0:T(8,128)}) %reduce-scatter.2.cloned.1.call-update) | async-done | bytes 393232 | tf_op jit(solution)/shard_map/reduce_scatter | solution.py:22
  123.6 1.3 reshape.111
  125.0 0.5 copy.31
  125.4 0.6 gather_fusion.3
  126.0 0.1 copy.32
  126.2 0.8 reshape.112
  (9 shorter events, 0.1 us)
Async XLA Ops:
  6.5 117.1 %reduce-scatter.2.cloned.1.call-start = ((), (), s32[]{:S(2)}) async-start(), calls=%async_computation.2 | async-start | bytes 1966080 | tf_op jit(solution)/shard_map/reduce_scatter | solution.py:22
  38.5 2.9 %copy-start = (s32[256]{0:T(256)S(1)}, s32[256]{0:T(256)}, u32[]{:S(2)}) copy-start(s32[256]{0:T(256)} %param.9) | copy-start | bytes 3076
  94.9 1.3 copy-start.2
  94.9 2.6 %copy-start.1 = (s32[24]{0:T(128)S(1)}, s32[24]{0:T(128)}, u32[]{:S(2)}) copy-start(s32[24]{0:T(128)} %param.8) | copy-start | bytes 292
Sparse Core Ops, SparseCore 0:
  96.3 27.2 reduce-scatter.1
where the time goes:
time: 135 us; the launch traced here: 134 us
  blocking collectives  49.2 us (36%)
  local copies, waits for them, and re-layouts  36.4 us (27%)
  waiting for transfers between devices  19.7 us (15%)
  between operations  14.2 us (11%)
  other arithmetic  7.28 us (5%)
  matrix products  7.1 us (5%)
    all_to_all x1, blocking collectives, local(): lax.all_to_all(partial_value, 'pair', split_axis=0, concat_axis=1, tiled=...  43.1 us
    reshape x2, local copies, waits for them, and re-layouts, local(): jnp.einsum('kli,ksj->ijkls', lam_coef, sig_coef)  23.5 us
    reduce_scatter x1, waiting for transfers between devices, local(): lax.psum_scatter(moved_rows, 'rng', scatter_dimension=0, tiled=True)  19.7 us
    dot_general x1, matrix products, local(): lax.dot_general(pair_cols, integrals, (((1,), (1,)), ((), ())), preferred...  7.1 us
    transpose x1, other arithmetic, local(): jnp.einsum('kli,ksj->ijkls', lam_coef, sig_coef)  6.25 us
    unnamed x1, blocking collectives  6.09 us
    gather x1, local copies, waits for them, and re-layouts, local(): pair_cols = pair_cols[pair_owner].astype(jnp.bfloat16)  3.2 us
  transfers between devices with their start and end apart: 1, of which 1 were waited for; matrix products, arithmetic and copies ran while one was open for 1% of the time, Pallas kernels for 0%

commit v1 on v0

v1 whole, which is shorter than its diff:
```python
import functools
import jax
import jax.numpy as jnp
from jax import lax
from jax.experimental import pallas as pl
from jax.experimental.pallas import tpu as pltpu
from jax.sharding import PartitionSpec as P

SHELL = 8
BLOCK_PAIRS = 64
NOCC = 16
NIJ = 256
LANES = 128
ROWS = 256
MIB = 1 << 20


def bits(size):
    return size.bit_length() - 1


def half_rows_kernel(
    pairs, ranges, shells, owner, coef, integrals, keep, send, table, lam, sig, cols, held, sems
):
    row_blocks = held.shape[0]
    kets = cols.shape[0] // BLOCK_PAIRS

    def fetch(step):
        return pltpu.make_async_copy(
            integrals.at[pl.ds(step * ROWS, ROWS), :], held.at[step], sems.at[step]
        )

    for step in range(row_blocks):
        fetch(step).start()

    me_pair, me_range = lax.axis_index("pair"), lax.axis_index("rng")
    rows_each = NIJ // (pairs * ranges)
    place = lax.broadcasted_iota(jnp.int32, (NIJ, NIJ), 1)
    inner = place % rows_each
    far_pair = (place // rows_each) % pairs
    order = place // (rows_each * pairs)
    far_range = jnp.zeros_like(order)
    for bit in range(bits(ranges)):
        far_range = far_range + (((order >> (bits(ranges) - 1 - bit)) & 1) << bit)
    target = ((far_pair ^ me_pair) * ranges + (far_range ^ me_range)) * rows_each + inner
    moved = (lax.broadcasted_iota(jnp.int32, (NIJ, NIJ), 0) == target).astype(jnp.bfloat16)
    orbital = lax.broadcasted_iota(jnp.int32, (NOCC, NIJ), 0)
    first = (owner[...] // NOCC == orbital).astype(jnp.bfloat16)
    second = (owner[...] % NOCC == orbital).astype(jnp.bfloat16)
    first = jnp.dot(first, moved, preferred_element_type=jnp.float32).astype(jnp.bfloat16)
    second = jnp.dot(second, moved, preferred_element_type=jnp.float32).astype(jnp.bfloat16)

    table[...] = coef[...].astype(jnp.float32).T

    for k in range(kets):
        here = pl.ds(k * SHELL, SHELL)
        lam[here, :NOCC] = table[pl.ds(pl.multiple_of(shells[0, k] * SHELL, SHELL), SHELL), :]
        sig[here, :NOCC] = table[pl.ds(pl.multiple_of(shells[1, k] * SHELL, SHELL), SHELL), :]
    lam[...] = jnp.dot(
        lam[:, :NOCC].astype(jnp.bfloat16), first, preferred_element_type=jnp.float32
    )
    sig[...] = jnp.dot(
        sig[:, :NOCC].astype(jnp.bfloat16), second, preferred_element_type=jnp.float32
    )
    for k in range(kets):
        here = pl.ds(k * SHELL, SHELL)
        both = lam[here, :][:, None, :] * sig[here, :][None, :, :]
        cols[pl.ds(k * BLOCK_PAIRS, BLOCK_PAIRS), :] = both.reshape(BLOCK_PAIRS, NIJ).astype(
            jnp.bfloat16
        )

    for step in range(row_blocks):
        fetch(step).wait()
        rows = jnp.dot(held[step], cols[...], preferred_element_type=jnp.float32).T
        here = pl.ds(step * ROWS, ROWS)
        keep[:, here] = rows[: NIJ // 2]
        send[:, here] = rows[NIJ // 2 :]


def half_rows(integrals, coefficients, ket_shells, pair_owner, pairs, ranges):
    rows, depth = integrals.shape
    kets = ket_shells.shape[0]
    half = jax.ShapeDtypeStruct((NIJ // 2, rows), jnp.float32)
    vmem = pl.BlockSpec(memory_space=pltpu.VMEM)
    return pl.pallas_call(
        functools.partial(half_rows_kernel, pairs, ranges),
        out_shape=(half, half),
        in_specs=[
            pl.BlockSpec(memory_space=pltpu.SMEM),
            vmem,
            vmem,
            pl.BlockSpec(memory_space=pl.ANY),
        ],
        out_specs=(vmem, vmem),
        scratch_shapes=[
            pltpu.VMEM((coefficients.shape[0], NOCC), jnp.float32),
            pltpu.VMEM((kets * SHELL, NIJ), jnp.float32),
            pltpu.VMEM((kets * SHELL, NIJ), jnp.float32),
            pltpu.VMEM((depth, NIJ), jnp.bfloat16),
            pltpu.VMEM((rows // ROWS, ROWS, depth), jnp.bfloat16),
            pltpu.SemaphoreType.DMA((rows // ROWS,)),
        ],
        compiler_params=pltpu.CompilerParams(vmem_limit_bytes=40 * MIB),
    )(ket_shells.T, pair_owner.reshape(1, NIJ), coefficients.T, integrals)


def place_kernel(slots, *refs):
    *pieces, out, numbers, scalars, sem = refs
    width = slots * BLOCK_PAIRS
    for d, piece in enumerate(pieces):
        numbers[pl.ds(d, 1), :] = piece[0:1, width:].astype(jnp.int32)
    copy = pltpu.make_async_copy(numbers, scalars, sem)
    copy.start()
    copy.wait()
    lane = lax.broadcasted_iota(jnp.int32, (out.shape[0], LANES), 1)
    upper = lane // BLOCK_PAIRS
    for d, piece in enumerate(pieces):
        for slot in range(slots):
            block = scalars[d, slot]
            side = slot % 2

            @pl.when(block >= 0)
            def _():
                value = piece[:, pl.ds((slot // 2) * LANES, LANES)]
                value = jnp.where(
                    block % 2 == side, value, pltpu.roll(value, BLOCK_PAIRS, 1)
                )
                there = pl.ds(pl.multiple_of((block // 2) * LANES, LANES), LANES)
                out[:, there] = jnp.where(upper == block % 2, value, out[:, there])


def placed_rows(pieces, slots, blocks):
    rows = pieces[0].shape[0]
    vmem = pl.BlockSpec(memory_space=pltpu.VMEM)
    return pl.pallas_call(
        functools.partial(place_kernel, slots),
        out_shape=jax.ShapeDtypeStruct((rows, blocks * BLOCK_PAIRS), jnp.float32),
        in_specs=[vmem] * len(pieces),
        out_specs=vmem,
        scratch_shapes=[
            pltpu.VMEM((len(pieces), LANES), jnp.int32),
            pltpu.SMEM((len(pieces), LANES), jnp.int32),
            pltpu.SemaphoreType.DMA,
        ],
    )(*pieces)


def swap(value, axis, size, far):
    return lax.ppermute(value, axis, [(i, i ^ far) for i in range(size)])


def local(pairs, ranges, integrals, coefficients, ket_shells, block_ids, pair_owner):
    slots = block_ids.shape[0]
    keep, send = half_rows(integrals, coefficients, ket_shells, pair_owner, pairs, ranges)
    rows = keep + swap(send, "rng", ranges, 1)
    each = NIJ // (pairs * ranges)
    rows = rows.reshape(ranges // 2, pairs, each, rows.shape[1])
    numbers = jnp.pad(block_ids.astype(jnp.float32), (0, LANES - slots))
    numbers = jnp.broadcast_to(numbers, (each, LANES))
    step = max(pairs // 2, 1)
    far = list(range(step, pairs)) + list(range(step))[::-1]
    pieces = [None] * pairs
    for start in range(0, pairs, step):
        group = far[start : start + step]
        part = jnp.stack([rows[:, d] for d in group], 1)
        for bit in range(1, bits(ranges)):
            half = part.shape[0] // 2
            part = part[:half] + swap(
                part[half:].reshape(-1, part.shape[-1]), "rng", ranges, 1 << bit
            ).reshape(part[half:].shape)
        for at, d in enumerate(group):
            piece = jnp.concatenate([part[0, at], numbers], axis=1)
            pieces[d] = swap(piece, "pair", pairs, d) if d else piece
    return placed_rows(pieces, slots, slots * pairs // 2)


def solution(mesh):
    placed = (
        P(("grp", "pair"), "rng"),
        P("grp", None),
        P(("grp", "rng"), None),
        P(("grp", "pair")),
        P(),
    )
    return jax.shard_map(
        functools.partial(local, mesh.shape["pair"], mesh.shape["rng"]),
        mesh=mesh,
        in_specs=placed,
        out_specs=P(("grp", "pair", "rng"), None),
        check_vma=False,
    )
```

time: 135 us -> 51.8 us (0.38)
  blocking collectives: 49.2 us -> 0 us
  local copies, waits for them, and re-layouts: 36.4 us -> 7.61 us
  Pallas kernels: 0 us -> 16 us
  between operations: 14.2 us -> 0.06 us
  starting transfers between devices: 0.01 us -> 7.95 us
  matrix products: 7.1 us -> 0 us
  other arithmetic: 7.28 us -> 0.87 us
    all_to_all x1 -> x0, blocking collectives: 43.1 us -> none  [local(): lax.all_to_all(partial_value, 'pair', split_axis=0, concat_axis=1, tiled=...]
    reshape x5 -> x0, local copies, waits for them, and re-layouts: 26.1 us -> none  [the longest x2 23.5 us: local(): jnp.einsum('kli,ksj->ijkls', lam_coef, sig_coef)]
    reduce_scatter x1 -> x0, waiting for transfers between devices: 19.7 us -> none  [local(): lax.psum_scatter(moved_rows, 'rng', scatter_dimension=0, tiled=True)]
    ppermute x0 -> x6, waiting for transfers between devices: none -> 19.1 us  [swap(): return lax.ppermute(value, axis, [(i, i ^ far) for i in range(size)])]
    pallas_call x0 -> x2, Pallas kernels: none -> 16 us  [the longest x1 10.2 us: half_rows(): pl.pallas_call(functools.partial(half_rows_kernel, pairs, ranges), out_sh...]
    ppermute x0 -> x6, starting transfers between devices: none -> 7.95 us  [swap(): return lax.ppermute(value, axis, [(i, i ^ far) for i in range(size)])]
    dot_general x1 -> x0, matrix products: 7.1 us -> none  [local(): lax.dot_general(pair_cols, integrals, (((1,), (1,)), ((), ())), preferred...]
    gather x5 -> x0, local copies, waits for them, and re-layouts: 6.62 us -> none  [the longest x1 3.2 us: local(): pair_cols = pair_cols[pair_owner].astype(jnp.bfloat16)]
  transfers between devices with their start and end apart: 1 -> 6, of which waited for: 1 -> 5; matrix products, arithmetic and copies ran while one was open for 1% -> 0% of each run, Pallas kernels for 0% -> 0%
where the time goes in v1:
time: 51.8 us; the launch traced here: 51.5 us
  waiting for transfers between devices  19.1 us (37%)
  Pallas kernels  16 us (31%)
  starting transfers between devices  7.95 us (15%)
  local copies, waits for them, and re-layouts  7.61 us (15%)
  other arithmetic  0.87 us (2%)
    ppermute x6, waiting for transfers between devices, swap(): return lax.ppermute(value, axis, [(i, i ^ far) for i in range(size)])  19.1 us
    pallas_call x1, Pallas kernels, half_rows(): pl.pallas_call(functools.partial(half_rows_kernel, pairs, ranges), out_sh...  10.2 us
    ppermute x6, starting transfers between devices, swap(): return lax.ppermute(value, axis, [(i, i ^ far) for i in range(size)])  7.95 us
    unnamed x16, local copies, waits for them, and re-layouts  7.53 us
    pallas_call x1, Pallas kernels, placed_rows(): pl.pallas_call(functools.partial(place_kernel, slots), out_shape=jax.Shap...  5.75 us
  transfers between devices with their start and end apart: 6, of which 5 were waited for; matrix products, arithmetic and copies ran while one was open for 0% of the time, Pallas kernels for 0%

profile of v1, /device:TPU:0, one launch (start us, length us, event | category | flops | bytes accessed | tf_op | source)
XLA Modules:
  0.0 51.5 jit_solution(6727980624055150246)
XLA Ops:
  0.0 0.0 copy-start.7
  0.0 0.0 copy-start
  0.0 4.6 %copy-done = bf16[1536,4096]{1,0:T(8,128)(2,1)S(1)} copy-done((bf16[1536,4096]{1,0:T(8,128)(2,1)S(1)}, bf16[1536,4096]{1,0:T(8,128)(2,1)}, u32[]{:S(2)}) %copy-start) | copy-done | bytes 12582936
  4.6 0.0 copy-start.1
  4.6 0.9 %copy-done.1 = bf16[4096,16]{0,1:T(8,128)(2,1)S(1)} copy-done((bf16[4096,16]{0,1:T(8,128)(2,1)S(1)}, bf16[4096,16]{0,1:T(8,128)(2,1)}, u32[]{:S(2)}) %copy-start.1) | copy-done | bytes 131096
  5.5 0.0 copy-start.2
  5.5 0.7 %copy-done.2 = s32[64,2]{0,1:T(2,128)S(1)} copy-done((s32[64,2]{0,1:T(2,128)S(1)}, s32[64,2]{0,1:T(2,128)}, u32[]{:S(2)}) %copy-start.2) | copy-done | bytes 536
  6.2 0.0 copy-start.3
  6.2 0.7 %copy-done.3 = s32[256]{0:T(256)S(1)} copy-done((s32[256]{0:T(256)S(1)}, s32[256]{0:T(256)}, u32[]{:S(2)}) %copy-start.3) | copy-done | bytes 1048
  6.9 10.2 %shard_map.55 = (f32[128,1536]{1,0:T(8,128)S(1)}, f32[128,1536]{1,0:T(8,128)S(1)}) custom-call(s32[2,64]{1,0:T(2,128)S(1)} %bitcast.17, s32[1,256]{1,0:T(1,128)S(1)} %bitcast.18, bf16[16,4096]{1,0:T(8,128)(2,1)S(1)} %bitcast.16, bf16[1536,4096]{1,0:T(8,128)(2,1)S(1)} %copy-done), custom_call_target="tpu_custom_call" | custom-call | tf_op jit(solution)/shard_map/pallas_call | solution.py:85
  17.1 0.5 collective-permute-start
  17.6 0.0 copy-done.7
  17.6 1.9 %collective-permute-done = f32[128,1536]{1,0:T(8,128)S(1)} collective-permute-done((f32[128,1536]{1,0:T(8,128)S(1)}, f32[128,1536]{1,0:T(8,128)S(1)}, u32[]{:S(2)}, u32[]{:S(2)}) %collective-permute-start) | collective-permute-done | bytes 786464 | tf_op jit(solution)/shard_map/ppermute | solution.py:149
  19.5 0.1 add.11
  19.7 2.9 %collective-permute-start.3 = (f32[32,1536]{1,0:T(8,128)S(1)}, f32[32,1536]{1,0:T(8,128)S(1)}, u32[]{:S(2)}, u32[]{:S(2)}) collective-permute-start(f32[32,1536]{1,0:T(8,128)S(1)} %bitcast.22), channel_id=1, source_target_pairs={{0,2},{1,3},{2,0},{3,1},{4,6},{5,7},{6,4},{7,5},{8,10},{9,11},{10,... | collective-permute-start | bytes 589832 | tf_op jit(solution)/shard_map/ppermute | solution.py:149
  22.6 0.1 collective-permute-start.1
  22.7 5.6 %collective-permute-done.3 = f32[32,1536]{1,0:T(8,128)S(1)} collective-permute-done((f32[32,1536]{1,0:T(8,128)S(1)}, f32[32,1536]{1,0:T(8,128)S(1)}, u32[]{:S(2)}, u32[]{:S(2)}) %collective-permute-start.3) | collective-permute-done | bytes 196640 | tf_op jit(solution)/shard_map/ppermute | solution.py:149
  28.3 3.7 %collective-permute-done.1 = f32[32,1536]{1,0:T(8,128)S(1)} collective-permute-done((f32[32,1536]{1,0:T(8,128)S(1)}, f32[32,1536]{1,0:T(8,128)S(1)}, u32[]{:S(2)}, u32[]{:S(2)}) %collective-permute-start.1) | collective-permute-done | bytes 196640 | tf_op jit(solution)/shard_map/ppermute | solution.py:149
  32.1 0.7 %pad_maximum_fusion.4 = (f32[16,1664]{1,0:T(8,128)S(1)}, f32[16,1664]{1,0:T(8,128)S(1)}, f32[16,1664]{1,0:T(8,128)S(1)}, f32[16,1664]{1,0:T(8,128)}) fusion(f32[16,1536]{1,0:T(8,128)S(1)} %get-tuple-element.11, f32[1664]{0:T(1024)S(1)} %pad_select_fusion, f32[16,1536]{1,0:T(8,128)S(1)} %get-tuple-element.20, f32[16,1536]{1,0:T(8,128)S(1)} %get-tuple-element.12, ...), kind=kLoop, calls=%fused_computation.9 | loop fusion | flops 106496 | bytes 825856 | tf_op jit(solution)/shard_map/concatenate | solution.py:172
  32.8 1.8 %collective-permute-start.2 = (f32[16,1664]{1,0:T(8,128)S(1)}, f32[16,1664]{1,0:T(8,128)S(1)}, u32[]{:S(2)}, u32[]{:S(2)}) collective-permute-start(f32[16,1664]{1,0:T(8,128)S(1)} %get-tuple-element.16), channel_id=1, source_target_pairs={{0,4},{4,0},{8,12},{12,8},{1,5},{5,1},{9,13},{13,9},{2,6},{6,2},{1... | collective-permute-start | bytes 319496 | tf_op jit(solution)/shard_map/ppermute | solution.py:149
  34.6 2.6 %collective-permute-start.4 = (f32[16,1664]{1,0:T(8,128)S(1)}, f32[16,1664]{1,0:T(8,128)S(1)}, u32[]{:S(2)}, u32[]{:S(2)}) collective-permute-start(f32[16,1664]{1,0:T(8,128)S(1)} %get-tuple-element.17), channel_id=1, source_target_pairs={{0,8},{4,12},{8,0},{12,4},{1,9},{5,13},{9,1},{13,5},{2,10},{6,14},... | collective-permute-start | bytes 319496 | tf_op jit(solution)/shard_map/ppermute | solution.py:149
  37.2 0.0 collective-permute-start.5
  37.2 1.3 %collective-permute-done.2.refs_1_ = f32[16,1664]{1,0:T(8,128)S(1)} collective-permute-done((f32[16,1664]{1,0:T(8,128)S(1)}, f32[16,1664]{1,0:T(8,128)S(1)}, u32[]{:S(2)}, u32[]{:S(2)}) %collective-permute-start.2) | collective-permute-done | bytes 106528 | tf_op jit(solution)/shard_map/ppermute | solution.py:149
  38.5 0.0 copy-start.4
  38.5 6.6 %collective-permute-done.4.refs_2_ = f32[16,1664]{1,0:T(8,128)S(1)} collective-permute-done((f32[16,1664]{1,0:T(8,128)S(1)}, f32[16,1664]{1,0:T(8,128)S(1)}, u32[]{:S(2)}, u32[]{:S(2)}) %collective-permute-start.4) | collective-permute-done | bytes 106528 | tf_op jit(solution)/shard_map/ppermute | solution.py:149
  45.1 0.0 copy-start.5
  45.1 0.0 collective-permute-done.5.refs_3_
  45.1 0.0 copy-start.6
  45.1 0.0 copy-done.4
  45.1 0.6 %copy-done.5 = f32[16,1664]{1,0:T(8,128)} copy-done((f32[16,1664]{1,0:T(8,128)}, f32[16,1664]{1,0:T(8,128)S(1)}, u32[]{:S(2)}) %copy-start.5) | copy-done | bytes 106520
  45.7 0.0 copy-done.6
  45.8 5.8 %shard_map.56 = f32[16,3072]{1,0:T(8,128)} custom-call(f32[16,1664]{1,0:T(8,128)} %get-tuple-element.18.refs_0_, f32[16,1664]{1,0:T(8,128)} %copy-done.4, f32[16,1664]{1,0:T(8,128)} %copy-done.5, f32[16,1664]{1,0:T(8,128)} %copy-done.6), custom_call_target="tpu_custom_call" | custom-call | tf_op jit(solution)/shard_map/pallas_call | solution.py:135
  (8 shorter events, 0.2 us)
Async XLA Ops:
  0.0 17.6 %copy-start.7 = (s32[24]{0:T(128)S(1)}, s32[24]{0:T(128)}, u32[]{:S(2)}) copy-start(s32[24]{0:T(128)} %param.8) | copy-start | bytes 292
  0.0 4.6 %copy-start = (bf16[1536,4096]{1,0:T(8,128)(2,1)S(1)}, bf16[1536,4096]{1,0:T(8,128)(2,1)}, u32[]{:S(2)}) copy-start(bf16[1536,4096]{1,0:T(8,128)(2,1)} %integrals.1) | copy-start | bytes 37748740
  4.6 0.9 %copy-start.1 = (bf16[4096,16]{0,1:T(8,128)(2,1)S(1)}, bf16[4096,16]{0,1:T(8,128)(2,1)}, u32[]{:S(2)}) copy-start(bf16[4096,16]{0,1:T(8,128)(2,1)} %param.6) | copy-start | bytes 393220
  5.5 0.7 %copy-start.2 = (s32[64,2]{0,1:T(2,128)S(1)}, s32[64,2]{0,1:T(2,128)}, u32[]{:S(2)}) copy-start(s32[64,2]{0,1:T(2,128)} %param.7) | copy-start | bytes 1540
  6.2 0.7 %copy-start.3 = (s32[256]{0:T(256)S(1)}, s32[256]{0:T(256)}, u32[]{:S(2)}) copy-start(s32[256]{0:T(256)} %param.9) | copy-start | bytes 3076
  17.1 2.4 %collective-permute-start = (f32[128,1536]{1,0:T(8,128)S(1)}, f32[128,1536]{1,0:T(8,128)S(1)}, u32[]{:S(2)}, u32[]{:S(2)}) collective-permute-start(f32[128,1536]{1,0:T(8,128)S(1)} %get-tuple-element.8), channel_id=1, source_target_pairs={{0,1},{1,0},{2,3},{3,2},{4,5},{5,4},{6,7},{7,6},{8,9},{9,8},{10,11... | collective-permute-start | bytes 2359304 | tf_op jit(solution)/shard_map/ppermute | solution.py:149
  19.7 8.6 %collective-permute-start.3 = (f32[32,1536]{1,0:T(8,128)S(1)}, f32[32,1536]{1,0:T(8,128)S(1)}, u32[]{:S(2)}, u32[]{:S(2)}) collective-permute-start(f32[32,1536]{1,0:T(8,128)S(1)} %bitcast.22), channel_id=1, source_target_pairs={{0,2},{1,3},{2,0},{3,1},{4,6},{5,7},{6,4},{7,5},{8,10},{9,11},{10,... | collective-permute-start | bytes 589832 | tf_op jit(solution)/shard_map/ppermute | solution.py:149
  22.6 9.4 %collective-permute-start.1 = (f32[32,1536]{1,0:T(8,128)S(1)}, f32[32,1536]{1,0:T(8,128)S(1)}, u32[]{:S(2)}, u32[]{:S(2)}) collective-permute-start(f32[32,1536]{1,0:T(8,128)S(1)} %bitcast.25), channel_id=1, source_target_pairs={{0,2},{1,3},{2,0},{3,1},{4,6},{5,7},{6,4},{7,5},{8,10},{9,11},{10,... | collective-permute-start | bytes 589832 | tf_op jit(solution)/shard_map/ppermute | solution.py:149
  32.8 5.8 %collective-permute-start.2 = (f32[16,1664]{1,0:T(8,128)S(1)}, f32[16,1664]{1,0:T(8,128)S(1)}, u32[]{:S(2)}, u32[]{:S(2)}) collective-permute-start(f32[16,1664]{1,0:T(8,128)S(1)} %get-tuple-element.16), channel_id=1, source_target_pairs={{0,4},{4,0},{8,12},{12,8},{1,5},{5,1},{9,13},{13,9},{2,6},{6,2},{1... | collective-permute-start | bytes 319496 | tf_op jit(solution)/shard_map/ppermute | solution.py:149
  34.6 10.5 %collective-permute-start.4 = (f32[16,1664]{1,0:T(8,128)S(1)}, f32[16,1664]{1,0:T(8,128)S(1)}, u32[]{:S(2)}, u32[]{:S(2)}) collective-permute-start(f32[16,1664]{1,0:T(8,128)S(1)} %get-tuple-element.17), channel_id=1, source_target_pairs={{0,8},{4,12},{8,0},{12,4},{1,9},{5,13},{9,1},{13,5},{2,10},{6,14},... | collective-permute-start | bytes 319496 | tf_op jit(solution)/shard_map/ppermute | solution.py:149
  37.2 7.9 %collective-permute-start.5 = (f32[16,1664]{1,0:T(8,128)S(1)}, f32[16,1664]{1,0:T(8,128)S(1)}, u32[]{:S(2)}, u32[]{:S(2)}) collective-permute-start(f32[16,1664]{1,0:T(8,128)S(1)} %get-tuple-element.15), channel_id=1, source_target_pairs={{0,12},{4,8},{8,4},{12,0},{1,13},{5,9},{9,5},{13,1},{2,14},{6,10},... | collective-permute-start | bytes 319496 | tf_op jit(solution)/shard_map/ppermute | solution.py:149
  38.5 6.6 %copy-start.4 = (f32[16,1664]{1,0:T(8,128)}, f32[16,1664]{1,0:T(8,128)S(1)}, u32[]{:S(2)}) copy-start(f32[16,1664]{1,0:T(8,128)S(1)} %collective-permute-done.2.refs_1_) | copy-start | bytes 319492
  45.1 0.6 %copy-start.5 = (f32[16,1664]{1,0:T(8,128)}, f32[16,1664]{1,0:T(8,128)S(1)}, u32[]{:S(2)}) copy-start(f32[16,1664]{1,0:T(8,128)S(1)} %collective-permute-done.4.refs_2_) | copy-start | bytes 319492
  45.1 0.7 %copy-start.6 = (f32[16,1664]{1,0:T(8,128)}, f32[16,1664]{1,0:T(8,128)S(1)}, u32[]{:S(2)}) copy-start(f32[16,1664]{1,0:T(8,128)S(1)} %collective-permute-done.5.refs_3_) | copy-start | bytes 319492

commit v2 on v1

v2 whole, which is shorter than its diff:
```python
import functools
import jax
import jax.numpy as jnp
from jax import lax
from jax.experimental import pallas as pl
from jax.experimental.pallas import tpu as pltpu
from jax.sharding import PartitionSpec as P

SHELL = 8
BLOCK_PAIRS = 64
NOCC = 16
NIJ = 256
LANES = 128
ROWS = 512
MIB = 1 << 20


def bits(size):
    return size.bit_length() - 1


def half_rows_kernel(
    pairs, ranges, shells_at, owner_at, coef_at, integrals, keep, send, shells, owner, coef,
    table, lam, sig, cols, held, small, sems,
):
    blocks = sems.shape[0]
    rows = held.shape[0] // blocks
    kets = cols.shape[0] // BLOCK_PAIRS

    def fetch(step):
        here = pl.ds(step * rows, rows)
        return pltpu.make_async_copy(integrals.at[here, :], held.at[here, :], sems.at[step])

    tables = [
        pltpu.make_async_copy(shells_at, shells, small.at[0]),
        pltpu.make_async_copy(owner_at, owner, small.at[1]),
        pltpu.make_async_copy(coef_at, coef, small.at[2]),
    ]
    for copy in tables:
        copy.start()
    for step in range(blocks):
        fetch(step).start()

    me_pair, me_range = lax.axis_index("pair"), lax.axis_index("rng")
    rows_each = NIJ // (pairs * ranges)
    place = lax.broadcasted_iota(jnp.int32, (SHELL, NIJ), 1)
    inner = place % rows_each
    far_pair = (place // rows_each) % pairs
    order = place // (rows_each * pairs)
    far_range = jnp.zeros_like(order)
    for bit in range(bits(ranges)):
        far_range = far_range + (((order >> (bits(ranges) - 1 - bit)) & 1) << bit)
    target = ((far_pair ^ me_pair) * ranges + (far_range ^ me_range)) * rows_each + inner
    moved = (lax.broadcasted_iota(jnp.int32, (NIJ, NIJ), 0) == target[0:1, :]).astype(jnp.bfloat16)
    orbital = lax.broadcasted_iota(jnp.int32, (NOCC, NIJ), 0)
    for copy in tables:
        copy.wait()
    picks = jnp.concatenate(
        [
            (owner[...] // NOCC == orbital).astype(jnp.bfloat16),
            (owner[...] % NOCC == orbital).astype(jnp.bfloat16),
        ],
        axis=0,
    )
    picks = jnp.dot(picks, moved, preferred_element_type=jnp.float32).astype(jnp.bfloat16)

    table[...] = coef[...].astype(jnp.float32).T

    for k in range(kets):
        here = pl.ds(k * SHELL, SHELL)
        lam[here, :NOCC] = table[pl.ds(pl.multiple_of(shells[0, k] * SHELL, SHELL), SHELL), :]
        sig[here, :NOCC] = table[pl.ds(pl.multiple_of(shells[1, k] * SHELL, SHELL), SHELL), :]
    lam[...] = jnp.dot(
        lam[:, :NOCC].astype(jnp.bfloat16), picks[:NOCC], preferred_element_type=jnp.float32
    )
    sig[...] = jnp.dot(
        sig[:, :NOCC].astype(jnp.bfloat16), picks[NOCC:], preferred_element_type=jnp.float32
    )
    for k in range(kets):
        here = pl.ds(k * SHELL, SHELL)
        both = lam[here, :][:, None, :] * sig[here, :][None, :, :]
        cols[pl.ds(k * BLOCK_PAIRS, BLOCK_PAIRS), :] = both.reshape(BLOCK_PAIRS, NIJ).astype(
            jnp.bfloat16
        )

    for step in range(blocks):
        fetch(step).wait()
        here = pl.ds(step * rows, rows)
        part = lax.dot_general(
            cols[...], held[here, :], (((0,), (1,)), ((), ())), preferred_element_type=jnp.float32
        )
        keep[:, here] = part[: NIJ // 2]
        send[:, here] = part[NIJ // 2 :]


def half_rows(integrals, coefficients, ket_shells, pair_owner, pairs, ranges):
    rows, depth = integrals.shape
    kets = ket_shells.shape[0]
    half = jax.ShapeDtypeStruct((NIJ // 2, rows), jnp.float32)
    vmem = pl.BlockSpec(memory_space=pltpu.VMEM)
    return pl.pallas_call(
        functools.partial(half_rows_kernel, pairs, ranges),
        out_shape=(half, half),
        in_specs=[pl.BlockSpec(memory_space=pl.ANY)] * 4,
        out_specs=(vmem, vmem),
        scratch_shapes=[
            pltpu.SMEM((2, kets), jnp.int32),
            pltpu.VMEM((1, NIJ), jnp.int32),
            pltpu.VMEM((NOCC, coefficients.shape[0]), jnp.bfloat16),
            pltpu.VMEM((coefficients.shape[0], NOCC), jnp.float32),
            pltpu.VMEM((kets * SHELL, NIJ), jnp.float32),
            pltpu.VMEM((kets * SHELL, NIJ), jnp.float32),
            pltpu.VMEM((depth, NIJ), jnp.bfloat16),
            pltpu.VMEM((rows, depth), jnp.bfloat16),
            pltpu.SemaphoreType.DMA((3,)),
            pltpu.SemaphoreType.DMA((rows // ROWS,)),
        ],
        compiler_params=pltpu.CompilerParams(vmem_limit_bytes=52 * MIB),
    )(ket_shells.T, pair_owner.reshape(1, NIJ), coefficients.T, integrals)


def place_kernel(slots, *refs):
    *pieces, out, numbers, scalars, sem = refs
    width = slots * BLOCK_PAIRS
    for d, piece in enumerate(pieces):
        numbers[pl.ds(d, 1), :] = piece[0:1, width:].astype(jnp.int32)
    copy = pltpu.make_async_copy(numbers, scalars, sem)
    copy.start()
    copy.wait()
    upper = lax.broadcasted_iota(jnp.int32, (out.shape[0], LANES), 1) // BLOCK_PAIRS
    for d, piece in enumerate(pieces):
        for tile in range(slots // 2):
            value = piece[:, tile * LANES : (tile + 1) * LANES]
            turned = pltpu.roll(value, BLOCK_PAIRS, 1)
            for side in range(2):
                block = scalars[d, 2 * tile + side]
                there = (jnp.maximum(block, 0) // 2) * LANES
                pltpu.store(
                    out.at[:, pl.ds(pl.multiple_of(there, LANES), LANES)],
                    jnp.where(block % 2 == side, value, turned),
                    mask=upper == jnp.where(block >= 0, block % 2, 2),
                )


def placed_rows(pieces, slots, blocks):
    rows = pieces[0].shape[0]
    vmem = pl.BlockSpec(memory_space=pltpu.VMEM)
    return pl.pallas_call(
        functools.partial(place_kernel, slots),
        out_shape=jax.ShapeDtypeStruct((rows, blocks * BLOCK_PAIRS), jnp.float32),
        in_specs=[vmem] * len(pieces),
        out_specs=vmem,
        scratch_shapes=[
            pltpu.VMEM((len(pieces), LANES), jnp.int32),
            pltpu.SMEM((len(pieces), LANES), jnp.int32),
            pltpu.SemaphoreType.DMA,
        ],
        compiler_params=pltpu.CompilerParams(vmem_limit_bytes=8 * MIB),
    )(*pieces)


def merge_kernel(count, mine_from, mine, theirs, ids, *outs):
    width = mine.shape[1]
    rows = outs[0].shape[0]
    for d in range(count):
        here = pl.ds(d * rows, rows)
        outs[d][:, :width] = mine[pl.ds(mine_from + d * rows, rows), :] + theirs[here, :]
        outs[d][:, width:] = jnp.broadcast_to(ids[...], (rows, LANES))


def merged(mine, mine_from, theirs, ids, count):
    vmem = pl.BlockSpec(memory_space=pltpu.VMEM)
    rows = theirs.shape[0] // count
    one = jax.ShapeDtypeStruct((rows, mine.shape[1] + LANES), jnp.float32)
    return pl.pallas_call(
        functools.partial(merge_kernel, count, mine_from),
        out_shape=[one] * count,
        in_specs=[vmem] * 3,
        out_specs=[vmem] * count,
        compiler_params=pltpu.CompilerParams(vmem_limit_bytes=8 * MIB),
    )(mine, theirs, ids)


def swap(value, axis, size, far):
    return lax.ppermute(value, axis, [(i, i ^ far) for i in range(size)])


def local(pairs, ranges, integrals, coefficients, ket_shells, block_ids, pair_owner):
    slots = block_ids.shape[0]
    keep, send = half_rows(integrals, coefficients, ket_shells, pair_owner, pairs, ranges)
    rows = keep + swap(send, "rng", ranges, 1)
    each = NIJ // (pairs * ranges)
    numbers = jnp.pad(block_ids.astype(jnp.float32), (0, LANES - slots)).reshape(1, LANES)
    pieces = [None] * pairs
    step = max(pairs // 2, 1)
    for first in range(0, pairs, step)[::-1]:
        last = first + step
        part = rows.reshape(ranges // 2, pairs, each, -1)[:, first:last]
        for bit in range(1, bits(ranges)):
            half = part.shape[0] // 2
            other = swap(part[half:].reshape(-1, part.shape[-1]), "rng", ranges, 1 << bit)
            if half > 1:
                part = part[:half] + other.reshape(part[half:].shape)
        parts = merged(rows[first * each : last * each], 0, other, numbers, last - first)
        for at in range(last - first):
            d = first + at
            pieces[d] = swap(parts[at], "pair", pairs, d) if d else parts[at]
    return placed_rows(pieces, slots, slots * pairs // 2)


def solution(mesh):
    placed = (
        P(("grp", "pair"), "rng"),
        P("grp", None),
        P(("grp", "rng"), None),
        P(("grp", "pair")),
        P(),
    )
    return jax.shard_map(
        functools.partial(local, mesh.shape["pair"], mesh.shape["rng"]),
        mesh=mesh,
        in_specs=placed,
        out_specs=P(("grp", "pair", "rng"), None),
        check_vma=False,
    )
```

time: 51.8 us -> 36.8 us (0.71)
  Pallas kernels: 16 us -> 8.33 us
  local copies, waits for them, and re-layouts: 7.61 us -> 2.34 us
  waiting for transfers between devices: 19.1 us -> 15.8 us
  starting transfers between devices: 7.95 us -> 9.99 us
  other arithmetic: 0.87 us -> 0.11 us
    unnamed x16 -> x8, local copies, waits for them, and re-layouts: 7.53 us -> 2.28 us
    pallas_call x1, Pallas kernels: 10.2 us -> 6.28 us  [half_rows(): pl.pallas_call(functools.partial(half_rows_kernel, pairs, ranges), out_sh...]
    pallas_call x1, Pallas kernels: 5.75 us -> 2.01 us  [placed_rows(): pl.pallas_call(functools.partial(place_kernel, slots), out_shape=jax.Shap...]
    ppermute x6, waiting for transfers between devices: 19.1 us -> 15.8 us  [swap(): return lax.ppermute(value, axis, [(i, i ^ far) for i in range(size)])]
    ppermute x6, starting transfers between devices: 7.95 us -> 9.99 us  [swap(): return lax.ppermute(value, axis, [(i, i ^ far) for i in range(size)])]
    concatenate x2 -> x0, other arithmetic: 0.69 us -> none  [local(): piece = jnp.concatenate([part[0, at], numbers], axis=1)]
  transfers between devices with their start and end apart: 6 -> 6, of which waited for: 5 -> 4; matrix products, arithmetic and copies ran while one was open for 0% -> 0% of each run, Pallas kernels for 0% -> 0%
where the time goes in v2:
time: 36.8 us; the launch traced here: 36.6 us
  waiting for transfers between devices  15.8 us (43%)
  starting transfers between devices  9.99 us (27%)
  Pallas kernels  8.33 us (23%)
  local copies, waits for them, and re-layouts  2.34 us (6%)
    ppermute x6, waiting for transfers between devices, swap(): return lax.ppermute(value, axis, [(i, i ^ far) for i in range(size)])  15.8 us
    ppermute x6, starting transfers between devices, swap(): return lax.ppermute(value, axis, [(i, i ^ far) for i in range(size)])  9.99 us
    pallas_call x1, Pallas kernels, half_rows(): pl.pallas_call(functools.partial(half_rows_kernel, pairs, ranges), out_sh...  6.28 us
    unnamed x8, local copies, waits for them, and re-layouts  2.28 us
    pallas_call x1, Pallas kernels, placed_rows(): pl.pallas_call(functools.partial(place_kernel, slots), out_shape=jax.Shap...  2.01 us
  transfers between devices with their start and end apart: 6, of which 4 were waited for; matrix products, arithmetic and copies ran while one was open for 0% of the time, Pallas kernels for 0%

profile of v2, /device:TPU:0, one launch (start us, length us, event | category | flops | bytes accessed | tf_op | source)
XLA Modules:
  0.0 36.6 jit_solution(15041693681518453735)
XLA Ops:
  0.0 0.0 copy-start.3
  0.0 0.0 copy-start
  0.0 0.9 %copy-done = bf16[4096,16]{0,1:T(8,128)(2,1)S(1)} copy-done((bf16[4096,16]{0,1:T(8,128)(2,1)S(1)}, bf16[4096,16]{0,1:T(8,128)(2,1)}, u32[]{:S(2)}) %copy-start) | copy-done | bytes 131096
  0.9 0.0 copy-start.1
  0.9 0.7 %copy-done.1 = s32[64,2]{0,1:T(2,128)S(1)} copy-done((s32[64,2]{0,1:T(2,128)S(1)}, s32[64,2]{0,1:T(2,128)}, u32[]{:S(2)}) %copy-start.1) | copy-done | bytes 536
  1.6 0.0 copy-start.2
  1.6 0.7 %copy-done.2 = s32[256]{0:T(256)S(1)} copy-done((s32[256]{0:T(256)S(1)}, s32[256]{0:T(256)}, u32[]{:S(2)}) %copy-start.2) | copy-done | bytes 1048
  2.3 6.3 %shard_map.55 = (f32[128,1536]{1,0:T(8,128)S(1)}, f32[128,1536]{1,0:T(8,128)S(1)}) custom-call(s32[2,64]{1,0:T(2,128)S(1)} %bitcast.9, s32[1,256]{1,0:T(1,128)S(1)} %bitcast.10, bf16[16,4096]{1,0:T(8,128)(2,1)S(1)} %bitcast.8, bf16[1536,4096]{1,0:T(8,128)(2,1)} %integrals.1), custom_call_target="tpu_custom_call" | custom-call | tf_op jit(solution)/shard_map/pallas_call | solution.py:101
  8.6 0.5 %collective-permute-start = (f32[128,1536]{1,0:T(8,128)S(1)}, f32[128,1536]{1,0:T(8,128)S(1)}, u32[]{:S(2)}, u32[]{:S(2)}) collective-permute-start(f32[128,1536]{1,0:T(8,128)S(1)} %get-tuple-element.12), channel_id=1, source_target_pairs={{0,1},{1,0},{2,3},{3,2},{4,5},{5,4},{6,7},{7,6},{8,9},{9,8},{10,11... | collective-permute-start | bytes 2359304 | tf_op jit(solution)/shard_map/ppermute | solution.py:185
  9.1 0.0 copy-done.3
  9.1 1.9 %collective-permute-done = f32[128,1536]{1,0:T(8,128)S(1)} collective-permute-done((f32[128,1536]{1,0:T(8,128)S(1)}, f32[128,1536]{1,0:T(8,128)S(1)}, u32[]{:S(2)}, u32[]{:S(2)}) %collective-permute-start) | collective-permute-done | bytes 786464 | tf_op jit(solution)/shard_map/ppermute | solution.py:185
  11.0 0.1 add.5
  11.1 2.9 %collective-permute-start.1 = (f32[32,1536]{1,0:T(8,128)S(1)}, f32[32,1536]{1,0:T(8,128)S(1)}, u32[]{:S(2)}, u32[]{:S(2)}) collective-permute-start(f32[32,1536]{1,0:T(8,128)S(1)} %bitcast.13), channel_id=1, source_target_pairs={{0,2},{1,3},{2,0},{3,1},{4,6},{5,7},{6,4},{7,5},{8,10},{9,11},{10,... | collective-permute-start | bytes 589832 | tf_op jit(solution)/shard_map/ppermute | solution.py:185
  14.1 0.1 collective-permute-start.3
  14.2 5.6 %collective-permute-done.1.theirs = f32[32,1536]{1,0:T(8,128)S(1)} collective-permute-done((f32[32,1536]{1,0:T(8,128)S(1)}, f32[32,1536]{1,0:T(8,128)S(1)}, u32[]{:S(2)}, u32[]{:S(2)}) %collective-permute-start.1) | collective-permute-done | bytes 196640 | tf_op jit(solution)/shard_map/ppermute | solution.py:185
  19.8 2.2 %collective-permute-start.2 = (f32[16,1664]{1,0:T(8,128)S(1)}, f32[16,1664]{1,0:T(8,128)S(1)}, u32[]{:S(2)}, u32[]{:S(2)}) collective-permute-start(f32[16,1664]{1,0:T(8,128)S(1)} %get-tuple-element.14), channel_id=1, source_target_pairs={{0,4},{4,0},{8,12},{12,8},{1,5},{5,1},{9,13},{13,9},{2,6},{6,2},{1... | collective-permute-start | bytes 319496 | tf_op jit(solution)/shard_map/ppermute | solution.py:185
  22.0 1.5 %collective-permute-done.3.theirs = f32[32,1536]{1,0:T(8,128)S(1)} collective-permute-done((f32[32,1536]{1,0:T(8,128)S(1)}, f32[32,1536]{1,0:T(8,128)S(1)}, u32[]{:S(2)}, u32[]{:S(2)}) %collective-permute-start.3) | collective-permute-done | bytes 196640 | tf_op jit(solution)/shard_map/ppermute | solution.py:185
  23.5 2.9 %collective-permute-start.4 = (f32[16,1664]{1,0:T(8,128)S(1)}, f32[16,1664]{1,0:T(8,128)S(1)}, u32[]{:S(2)}, u32[]{:S(2)}) collective-permute-start(f32[16,1664]{1,0:T(8,128)S(1)} %get-tuple-element.15), channel_id=1, source_target_pairs={{0,8},{4,12},{8,0},{12,4},{1,9},{5,13},{9,1},{13,5},{2,10},{6,14},... | collective-permute-start | bytes 319496 | tf_op jit(solution)/shard_map/ppermute | solution.py:185
  26.4 1.3 %collective-permute-start.5 = (f32[16,1664]{1,0:T(8,128)S(1)}, f32[16,1664]{1,0:T(8,128)S(1)}, u32[]{:S(2)}, u32[]{:S(2)}) collective-permute-start(f32[16,1664]{1,0:T(8,128)S(1)} %get-tuple-element.16), channel_id=1, source_target_pairs={{0,12},{4,8},{8,4},{12,0},{1,13},{5,9},{9,5},{13,1},{2,14},{6,10},... | collective-permute-start | bytes 319496 | tf_op jit(solution)/shard_map/ppermute | solution.py:185
  27.8 0.0 collective-permute-done.2.refs_1_
  27.8 6.8 %collective-permute-done.4.refs_2_ = f32[16,1664]{1,0:T(8,128)S(1)} collective-permute-done((f32[16,1664]{1,0:T(8,128)S(1)}, f32[16,1664]{1,0:T(8,128)S(1)}, u32[]{:S(2)}, u32[]{:S(2)}) %collective-permute-start.4) | collective-permute-done | bytes 106528 | tf_op jit(solution)/shard_map/ppermute | solution.py:185
  34.6 0.0 collective-permute-done.5.refs_3_
  34.6 2.0 %shard_map.58 = f32[16,3072]{1,0:T(8,128)} custom-call(f32[16,1664]{1,0:T(8,128)S(1)} %get-tuple-element.13.refs_0_, f32[16,1664]{1,0:T(8,128)S(1)} %collective-permute-done.2.refs_1_, f32[16,1664]{1,0:T(8,128)S(1)} %collective-permute-done.4.refs_2_, f32[16,1664]{1,0:T(8,128)S(1)} %collective-permute-done.5.refs_3_), custom_call_target="tpu_custom_call" | custom-call | tf_op jit(solution)/shard_map/pallas_call | solution.py:148
  (6 shorter events, 0.1 us)
Async XLA Ops:
  0.0 9.1 %copy-start.3 = (s32[24]{0:T(128)S(1)}, s32[24]{0:T(128)}, u32[]{:S(2)}) copy-start(s32[24]{0:T(128)} %param.8) | copy-start | bytes 292
  0.0 0.9 %copy-start = (bf16[4096,16]{0,1:T(8,128)(2,1)S(1)}, bf16[4096,16]{0,1:T(8,128)(2,1)}, u32[]{:S(2)}) copy-start(bf16[4096,16]{0,1:T(8,128)(2,1)} %param.6) | copy-start | bytes 393220
  0.9 0.7 %copy-start.1 = (s32[64,2]{0,1:T(2,128)S(1)}, s32[64,2]{0,1:T(2,128)}, u32[]{:S(2)}) copy-start(s32[64,2]{0,1:T(2,128)} %param.7) | copy-start | bytes 1540
  1.6 0.7 %copy-start.2 = (s32[256]{0:T(256)S(1)}, s32[256]{0:T(256)}, u32[]{:S(2)}) copy-start(s32[256]{0:T(256)} %param.9) | copy-start | bytes 3076
  8.6 2.4 %collective-permute-start = (f32[128,1536]{1,0:T(8,128)S(1)}, f32[128,1536]{1,0:T(8,128)S(1)}, u32[]{:S(2)}, u32[]{:S(2)}) collective-permute-start(f32[128,1536]{1,0:T(8,128)S(1)} %get-tuple-element.12), channel_id=1, source_target_pairs={{0,1},{1,0},{2,3},{3,2},{4,5},{5,4},{6,7},{7,6},{8,9},{9,8},{10,11... | collective-permute-start | bytes 2359304 | tf_op jit(solution)/shard_map/ppermute | solution.py:185
  11.1 8.6 %collective-permute-start.1 = (f32[32,1536]{1,0:T(8,128)S(1)}, f32[32,1536]{1,0:T(8,128)S(1)}, u32[]{:S(2)}, u32[]{:S(2)}) collective-permute-start(f32[32,1536]{1,0:T(8,128)S(1)} %bitcast.13), channel_id=1, source_target_pairs={{0,2},{1,3},{2,0},{3,1},{4,6},{5,7},{6,4},{7,5},{8,10},{9,11},{10,... | collective-permute-start | bytes 589832 | tf_op jit(solution)/shard_map/ppermute | solution.py:185
  14.1 9.4 %collective-permute-start.3 = (f32[32,1536]{1,0:T(8,128)S(1)}, f32[32,1536]{1,0:T(8,128)S(1)}, u32[]{:S(2)}, u32[]{:S(2)}) collective-permute-start(f32[32,1536]{1,0:T(8,128)S(1)} %bitcast.12), channel_id=1, source_target_pairs={{0,2},{1,3},{2,0},{3,1},{4,6},{5,7},{6,4},{7,5},{8,10},{9,11},{10,... | collective-permute-start | bytes 589832 | tf_op jit(solution)/shard_map/ppermute | solution.py:185
  19.8 8.0 %collective-permute-start.2 = (f32[16,1664]{1,0:T(8,128)S(1)}, f32[16,1664]{1,0:T(8,128)S(1)}, u32[]{:S(2)}, u32[]{:S(2)}) collective-permute-start(f32[16,1664]{1,0:T(8,128)S(1)} %get-tuple-element.14), channel_id=1, source_target_pairs={{0,4},{4,0},{8,12},{12,8},{1,5},{5,1},{9,13},{13,9},{2,6},{6,2},{1... | collective-permute-start | bytes 319496 | tf_op jit(solution)/shard_map/ppermute | solution.py:185
  23.5 11.1 %collective-permute-start.4 = (f32[16,1664]{1,0:T(8,128)S(1)}, f32[16,1664]{1,0:T(8,128)S(1)}, u32[]{:S(2)}, u32[]{:S(2)}) collective-permute-start(f32[16,1664]{1,0:T(8,128)S(1)} %get-tuple-element.15), channel_id=1, source_target_pairs={{0,8},{4,12},{8,0},{12,4},{1,9},{5,13},{9,1},{13,5},{2,10},{6,14},... | collective-permute-start | bytes 319496 | tf_op jit(solution)/shard_map/ppermute | solution.py:185
  26.4 8.2 %collective-permute-start.5 = (f32[16,1664]{1,0:T(8,128)S(1)}, f32[16,1664]{1,0:T(8,128)S(1)}, u32[]{:S(2)}, u32[]{:S(2)}) collective-permute-start(f32[16,1664]{1,0:T(8,128)S(1)} %get-tuple-element.16), channel_id=1, source_target_pairs={{0,12},{4,8},{8,4},{12,0},{1,13},{5,9},{9,5},{13,1},{2,14},{6,10},... | collective-permute-start | bytes 319496 | tf_op jit(solution)/shard_map/ppermute | solution.py:185

commit v3 on v2

--- a/solution.py
+++ b/solution.py
@@ -11,7 +11,7 @@
 NOCC = 16
 NIJ = 256
 LANES = 128
-ROWS = 512
+STEPS = 4
 MIB = 1 << 20
 
 
@@ -19,28 +19,7 @@
     return size.bit_length() - 1
 
 
-def half_rows_kernel(
-    pairs, ranges, shells_at, owner_at, coef_at, integrals, keep, send, shells, owner, coef,
-    table, lam, sig, cols, held, small, sems,
-):
-    blocks = sems.shape[0]
-    rows = held.shape[0] // blocks
-    kets = cols.shape[0] // BLOCK_PAIRS
-
-    def fetch(step):
-        here = pl.ds(step * rows, rows)
-        return pltpu.make_async_copy(integrals.at[here, :], held.at[here, :], sems.at[step])
-
-    tables = [
-        pltpu.make_async_copy(shells_at, shells, small.at[0]),
-        pltpu.make_async_copy(owner_at, owner, small.at[1]),
-        pltpu.make_async_copy(coef_at, coef, small.at[2]),
-    ]
-    for copy in tables:
-        copy.start()
-    for step in range(blocks):
-        fetch(step).start()
-
+def order_kernel(pairs, ranges, moved):
     me_pair, me_range = lax.axis_index("pair"), lax.axis_index("rng")
     rows_each = NIJ // (pairs * ranges)
     place = lax.broadcasted_iota(jnp.int32, (SHELL, NIJ), 1)
@@ -51,7 +30,42 @@
     for bit in range(bits(ranges)):
         far_range = far_range + (((order >> (bits(ranges) - 1 - bit)) & 1) << bit)
     target = ((far_pair ^ me_pair) * ranges + (far_range ^ me_range)) * rows_each + inner
-    moved = (lax.broadcasted_iota(jnp.int32, (NIJ, NIJ), 0) == target[0:1, :]).astype(jnp.bfloat16)
+    row = lax.broadcasted_iota(jnp.int32, (NIJ, NIJ), 0)
+    moved[...] = (row == target[0:1, :]).astype(jnp.bfloat16)
+
+
+def order_of(pairs, ranges):
+    return pl.pallas_call(
+        functools.partial(order_kernel, pairs, ranges),
+        out_shape=jax.ShapeDtypeStruct((NIJ, NIJ), jnp.bfloat16),
+        out_specs=pl.BlockSpec(memory_space=pltpu.VMEM),
+        compiler_params=pltpu.CompilerParams(vmem_limit_bytes=8 * MIB),
+        cost_estimate=pl.CostEstimate(flops=10**10, bytes_accessed=NIJ * NIJ * 2, transcendentals=0),
+    )()
+
+
+def half_rows_kernel(
+    shells_at, owner_at, coef_at, moved, integrals, keep, send, shells, owner, coef,
+    table, lam, sig, cols, held, small, sems,
+):
+    steps = sems.shape[0]
+    depth = held.shape[1] // steps
+    kets = cols.shape[0] // BLOCK_PAIRS
+
+    def fetch(step):
+        here = pl.ds(step * depth, depth)
+        return pltpu.make_async_copy(integrals.at[:, here], held.at[:, here], sems.at[step])
+
+    tables = [
+        pltpu.make_async_copy(shells_at, shells, small.at[0]),
+        pltpu.make_async_copy(owner_at, owner, small.at[1]),
+        pltpu.make_async_copy(coef_at, coef, small.at[2]),
+    ]
+    for copy in tables:
+        copy.start()
+    for step in range(steps):
+        fetch(step).start()
+
     orbital = lax.broadcasted_iota(jnp.int32, (NOCC, NIJ), 0)
     for copy in tables:
         copy.wait()
@@ -62,7 +76,7 @@
         ],
         axis=0,
     )
-    picks = jnp.dot(picks, moved, preferred_element_type=jnp.float32).astype(jnp.bfloat16)
+    picks = jnp.dot(picks, moved[...], preferred_element_type=jnp.float32).astype(jnp.bfloat16)
 
     table[...] = coef[...].astype(jnp.float32).T
 
@@ -76,21 +90,23 @@
     sig[...] = jnp.dot(
         sig[:, :NOCC].astype(jnp.bfloat16), picks[NOCC:], preferred_element_type=jnp.float32
     )
-    for k in range(kets):
-        here = pl.ds(k * SHELL, SHELL)
-        both = lam[here, :][:, None, :] * sig[here, :][None, :, :]
-        cols[pl.ds(k * BLOCK_PAIRS, BLOCK_PAIRS), :] = both.reshape(BLOCK_PAIRS, NIJ).astype(
-            jnp.bfloat16
+    each = kets // steps
+    for step in range(steps):
+        for k in range(step * each, (step + 1) * each):
+            here = pl.ds(k * SHELL, SHELL)
+            both = lam[here, :][:, None, :] * sig[here, :][None, :, :]
+            cols[pl.ds(k * BLOCK_PAIRS, BLOCK_PAIRS), :] = both.reshape(BLOCK_PAIRS, NIJ).astype(
+                jnp.bfloat16
+            )
+        fetch(step).wait()
+        here = pl.ds(step * depth, depth)
+        part = lax.dot_general(
+            cols[here, :], held[:, here], (((0,), (1,)), ((), ())),
+            preferred_element_type=jnp.float32,
         )
-
-    for step in range(blocks):
-        fetch(step).wait()
-        here = pl.ds(step * rows, rows)
-        part = lax.dot_general(
-            cols[...], held[here, :], (((0,), (1,)), ((), ())), preferred_element_type=jnp.float32
-        )
-        keep[:, here] = part[: NIJ // 2]
-        send[:, here] = part[NIJ // 2 :]
+        for at, out in enumerate((keep, send)):
+            half = part[at * (NIJ // 2) : (at + 1) * (NIJ // 2)]
+            out[...] = half if step == 0 else out[...] + half
 
 
 def half_rows(integrals, coefficients, ket_shells, pair_owner, pairs, ranges):
@@ -99,9 +115,10 @@
     half = jax.ShapeDtypeStruct((NIJ // 2, rows), jnp.float32)
     vmem = pl.BlockSpec(memory_space=pltpu.VMEM)
     return pl.pallas_call(
-        functools.partial(half_rows_kernel, pairs, ranges),
+        half_rows_kernel,
         out_shape=(half, half),
-        in_specs=[pl.BlockSpec(memory_space=pl.ANY)] * 4,
+        in_specs=[pl.BlockSpec(memory_space=pl.ANY)] * 3
+        + [vmem, pl.BlockSpec(memory_space=pl.ANY)],
         out_specs=(vmem, vmem),
         scratch_shapes=[
             pltpu.SMEM((2, kets), jnp.int32),
@@ -113,10 +130,10 @@
             pltpu.VMEM((depth, NIJ), jnp.bfloat16),
             pltpu.VMEM((rows, depth), jnp.bfloat16),
             pltpu.SemaphoreType.DMA((3,)),
-            pltpu.SemaphoreType.DMA((rows // ROWS,)),
+            pltpu.SemaphoreType.DMA((STEPS,)),
         ],
         compiler_params=pltpu.CompilerParams(vmem_limit_bytes=52 * MIB),
-    )(ket_shells.T, pair_owner.reshape(1, NIJ), coefficients.T, integrals)
+    )(ket_shells.T, pair_owner.reshape(1, NIJ), coefficients.T, order_of(pairs, ranges), integrals)
 
 
 def place_kernel(slots, *refs):
@@ -159,7 +176,28 @@
     )(*pieces)
 
 
-def merge_kernel(count, mine_from, mine, theirs, ids, *outs):
+def sum_kernel(spans, mine, theirs, earlier, lower, upper):
+    half = len(spans) // 2
+    for at, (start, size) in enumerate(spans):
+        out, place = (lower, at) if at < half else (upper, at - half)
+        here = pl.ds(start, size)
+        out[pl.ds(place * size, size), :] = mine[here, :] + theirs[here, :]
+
+
+def summed(mine, theirs, earlier, spans):
+    vmem = pl.BlockSpec(memory_space=pltpu.VMEM)
+    rows = sum(size for _, size in spans) // 2
+    half = jax.ShapeDtypeStruct((rows, mine.shape[1]), jnp.float32)
+    return pl.pallas_call(
+        functools.partial(sum_kernel, spans),
+        out_shape=[half] * 2,
+        in_specs=[vmem] * 2 + [pl.BlockSpec(memory_space=pl.ANY)],
+        out_specs=[vmem] * 2,
+        compiler_params=pltpu.CompilerParams(vmem_limit_bytes=8 * MIB),
+    )(mine, theirs, earlier)
+
+
+def merge_kernel(count, mine_from, mine, theirs, ids, earlier, *outs):
     width = mine.shape[1]
     rows = outs[0].shape[0]
     for d in range(count):
@@ -168,17 +206,17 @@
         outs[d][:, width:] = jnp.broadcast_to(ids[...], (rows, LANES))
 
 
-def merged(mine, mine_from, theirs, ids, count):
+def merged(mine, mine_from, theirs, ids, earlier, count):
     vmem = pl.BlockSpec(memory_space=pltpu.VMEM)
     rows = theirs.shape[0] // count
     one = jax.ShapeDtypeStruct((rows, mine.shape[1] + LANES), jnp.float32)
     return pl.pallas_call(
         functools.partial(merge_kernel, count, mine_from),
         out_shape=[one] * count,
-        in_specs=[vmem] * 3,
+        in_specs=[vmem] * 3 + [pl.BlockSpec(memory_space=pl.ANY)],
         out_specs=[vmem] * count,
         compiler_params=pltpu.CompilerParams(vmem_limit_bytes=8 * MIB),
-    )(mine, theirs, ids)
+    )(mine, theirs, ids, earlier)
 
 
 def swap(value, axis, size, far):
@@ -188,23 +226,32 @@
 def local(pairs, ranges, integrals, coefficients, ket_shells, block_ids, pair_owner):
     slots = block_ids.shape[0]
     keep, send = half_rows(integrals, coefficients, ket_shells, pair_owner, pairs, ranges)
-    rows = keep + swap(send, "rng", ranges, 1)
+    across = swap(send, "rng", ranges, 1)
     each = NIJ // (pairs * ranges)
     numbers = jnp.pad(block_ids.astype(jnp.float32), (0, LANES - slots)).reshape(1, LANES)
+    step = max(pairs // 2, 1)
+    size = step * each
+    halves = []
+    earlier = across
+    for first in range(0, pairs, step)[::-1]:
+        spans = tuple(((o * pairs + first) * each, size) for o in range(ranges // 2))
+        lower, upper = summed(keep, across, earlier, spans)
+        halves.append((first, lower, upper))
+        earlier = lower
     pieces = [None] * pairs
-    step = max(pairs // 2, 1)
-    for first in range(0, pairs, step)[::-1]:
-        last = first + step
-        part = rows.reshape(ranges // 2, pairs, each, -1)[:, first:last]
+    earlier = numbers
+    for first, lower, upper in halves:
         for bit in range(1, bits(ranges)):
-            half = part.shape[0] // 2
-            other = swap(part[half:].reshape(-1, part.shape[-1]), "rng", ranges, 1 << bit)
-            if half > 1:
-                part = part[:half] + other.reshape(part[half:].shape)
-        parts = merged(rows[first * each : last * each], 0, other, numbers, last - first)
-        for at in range(last - first):
+            other = swap(upper, "rng", ranges, 1 << bit)
+            if bit < bits(ranges) - 1:
+                lower = lower + other
+                lower, upper = jnp.split(lower, 2)
+        parts = merged(lower, 0, other, numbers, earlier, step)
+        earlier = parts[0]
+        for at in range(step):
             d = first + at
             pieces[d] = swap(parts[at], "pair", pairs, d) if d else parts[at]
+    pieces = pieces[:1] + pieces[step:] + pieces[1:step]
     return placed_rows(pieces, slots, slots * pairs // 2)
 
 

time: 36.8 us -> 31.5 us (0.86)
  waiting for transfers between devices: 15.8 us -> 12.9 us
  local copies, waits for them, and re-layouts: 2.34 us -> 0.89 us
  starting transfers between devices: 9.99 us -> 9.11 us
    ppermute x6, waiting for transfers between devices: 15.8 us -> 12.9 us  [swap(): return lax.ppermute(value, axis, [(i, i ^ far) for i in range(size)])]
    unnamed x8, local copies, waits for them, and re-layouts: 2.28 us -> 0.89 us
    ppermute x6, starting transfers between devices: 9.99 us -> 9.11 us  [swap(): return lax.ppermute(value, axis, [(i, i ^ far) for i in range(size)])]
    pallas_call x1 -> x4, Pallas kernels: 6.28 us -> 6.3 us  [the longest x1 6.16 us: half_rows(): pl.pallas_call(half_rows_kernel, out_shape=(half, half), in_specs=[pl.Blo...]
where the time goes in v3:
time: 31.5 us; the launch traced here: 31.4 us
  waiting for transfers between devices  12.9 us (41%)
  starting transfers between devices  9.11 us (29%)
  Pallas kernels  8.36 us (27%)
  local copies, waits for them, and re-layouts  0.89 us (3%)
    ppermute x6, waiting for transfers between devices, swap(): return lax.ppermute(value, axis, [(i, i ^ far) for i in range(size)])  12.9 us
    ppermute x6, starting transfers between devices, swap(): return lax.ppermute(value, axis, [(i, i ^ far) for i in range(size)])  9.11 us
    pallas_call x1, Pallas kernels, half_rows(): pl.pallas_call(half_rows_kernel, out_shape=(half, half), in_specs=[pl.Blo...  6.16 us
    pallas_call x1, Pallas kernels, placed_rows(): pl.pallas_call(functools.partial(place_kernel, slots), out_shape=jax.Shap...  2.01 us
    unnamed x8, local copies, waits for them, and re-layouts  0.89 us
  transfers between devices with their start and end apart: 6, of which 4 were waited for; matrix products, arithmetic and copies ran while one was open for 0% of the time, Pallas kernels for 0%

profile of v3, /device:TPU:0, one launch (start us, length us, event | category | flops | bytes accessed | tf_op | source)
XLA Modules:
  0.0 31.4 jit_solution(14235052931459459336)
XLA Ops:
  0.0 0.0 copy-start.1
  0.0 0.0 copy-start.2
  0.0 0.0 copy-start
  0.0 0.0 copy-start.3
  0.1 0.6 %copy-done.1 = s32[64,2]{0,1:T(2,128)S(1)} copy-done((s32[64,2]{0,1:T(2,128)S(1)}, s32[64,2]{0,1:T(2,128)}, u32[]{:S(2)}) %copy-start.1) | copy-done | bytes 536
  0.7 0.0 copy-done.2
  0.7 0.2 copy-done
  0.9 6.2 %shard_map.56 = (f32[128,1536]{1,0:T(8,128)S(1)}, f32[128,1536]{1,0:T(8,128)S(1)}) custom-call(s32[2,64]{1,0:T(2,128)S(1)} %bitcast.6, s32[1,256]{1,0:T(1,128)S(1)} %bitcast.7, bf16[16,4096]{1,0:T(8,128)(2,1)S(1)} %bitcast.5, bf16[256,256]{1,0:T(8,128)(2,1)S(1)} %shard_map.55.moved, bf16[1536,4096]{1,0:T(8,128)(2,1)} %integrals.1), custom_call_target="tpu_custom_call" | custom-call | tf_op jit(solution)/shard_map/pallas_call | solution.py:117
  7.1 0.5 %collective-permute-start = (f32[128,1536]{1,0:T(8,128)S(1)}, f32[128,1536]{1,0:T(8,128)S(1)}, u32[]{:S(2)}, u32[]{:S(2)}) collective-permute-start(f32[128,1536]{1,0:T(8,128)S(1)} %get-tuple-element.16), channel_id=1, source_target_pairs={{0,1},{1,0},{2,3},{3,2},{4,5},{5,4},{6,7},{7,6},{8,9},{9,8},{10,11... | collective-permute-start | bytes 2359304 | tf_op jit(solution)/shard_map/ppermute | solution.py:223
  7.6 1.9 %collective-permute-done.theirs.earlier = f32[128,1536]{1,0:T(8,128)S(1)} collective-permute-done((f32[128,1536]{1,0:T(8,128)S(1)}, f32[128,1536]{1,0:T(8,128)S(1)}, u32[]{:S(2)}, u32[]{:S(2)}) %collective-permute-start) | collective-permute-done | bytes 786464 | tf_op jit(solution)/shard_map/ppermute | solution.py:223
  9.5 0.1 shard_map.57
  9.6 2.9 %collective-permute-start.2 = (f32[32,1536]{1,0:T(8,128)S(1)}, f32[32,1536]{1,0:T(8,128)S(1)}, u32[]{:S(2)}, u32[]{:S(2)}) collective-permute-start(f32[32,1536]{1,0:T(8,128)S(1)} %get-tuple-element.20), channel_id=1, source_target_pairs={{0,2},{1,3},{2,0},{3,1},{4,6},{5,7},{6,4},{7,5},{8,10},{9,11},{10,... | collective-permute-start | bytes 589832 | tf_op jit(solution)/shard_map/ppermute | solution.py:223
  12.5 0.1 shard_map.58
  12.6 0.1 collective-permute-start.1
  12.6 0.0 copy-done.3
  12.7 5.5 %collective-permute-done.2.theirs = f32[32,1536]{1,0:T(8,128)S(1)} collective-permute-done((f32[32,1536]{1,0:T(8,128)S(1)}, f32[32,1536]{1,0:T(8,128)S(1)}, u32[]{:S(2)}, u32[]{:S(2)}) %collective-permute-start.2) | collective-permute-done | bytes 196640 | tf_op jit(solution)/shard_map/ppermute | solution.py:223
  18.2 3.2 %collective-permute-start.3 = (f32[16,1664]{1,0:T(8,128)S(1)}, f32[16,1664]{1,0:T(8,128)S(1)}, u32[]{:S(2)}, u32[]{:S(2)}) collective-permute-start(f32[16,1664]{1,0:T(8,128)S(1)} %get-tuple-element.21.earlier), channel_id=1, source_target_pairs={{0,8},{4,12},{8,0},{12,4},{1,9},{5,13},{9,1},{13,5},{2,10},{6,14},... | collective-permute-start | bytes 319496 | tf_op jit(solution)/shard_map/ppermute | solution.py:223
  21.4 1.3 %collective-permute-start.4 = (f32[16,1664]{1,0:T(8,128)S(1)}, f32[16,1664]{1,0:T(8,128)S(1)}, u32[]{:S(2)}, u32[]{:S(2)}) collective-permute-start(f32[16,1664]{1,0:T(8,128)S(1)} %get-tuple-element.23), channel_id=1, source_target_pairs={{0,12},{4,8},{8,4},{12,0},{1,13},{5,9},{9,5},{13,1},{2,14},{6,10},... | collective-permute-start | bytes 319496 | tf_op jit(solution)/shard_map/ppermute | solution.py:223
  22.8 0.0 collective-permute-done.1.theirs
  22.8 1.0 %collective-permute-start.5 = (f32[16,1664]{1,0:T(8,128)S(1)}, f32[16,1664]{1,0:T(8,128)S(1)}, u32[]{:S(2)}, u32[]{:S(2)}) collective-permute-start(f32[16,1664]{1,0:T(8,128)S(1)} %get-tuple-element.24), channel_id=1, source_target_pairs={{0,4},{4,0},{8,12},{12,8},{1,5},{5,1},{9,13},{13,9},{2,6},{6,2},{1... | collective-permute-start | bytes 319496 | tf_op jit(solution)/shard_map/ppermute | solution.py:223
  23.9 5.0 %collective-permute-done.3.refs_1_ = f32[16,1664]{1,0:T(8,128)S(1)} collective-permute-done((f32[16,1664]{1,0:T(8,128)S(1)}, f32[16,1664]{1,0:T(8,128)S(1)}, u32[]{:S(2)}, u32[]{:S(2)}) %collective-permute-start.3) | collective-permute-done | bytes 106528 | tf_op jit(solution)/shard_map/ppermute | solution.py:223
  28.8 0.0 collective-permute-done.4.refs_2_
  28.8 0.5 %collective-permute-done.5.refs_3_ = f32[16,1664]{1,0:T(8,128)S(1)} collective-permute-done((f32[16,1664]{1,0:T(8,128)S(1)}, f32[16,1664]{1,0:T(8,128)S(1)}, u32[]{:S(2)}, u32[]{:S(2)}) %collective-permute-start.5) | collective-permute-done | bytes 106528 | tf_op jit(solution)/shard_map/ppermute | solution.py:223
  29.4 2.0 %shard_map.61 = f32[16,3072]{1,0:T(8,128)} custom-call(f32[16,1664]{1,0:T(8,128)S(1)} %get-tuple-element.22.refs_0_, f32[16,1664]{1,0:T(8,128)S(1)} %collective-permute-done.3.refs_1_, f32[16,1664]{1,0:T(8,128)S(1)} %collective-permute-done.4.refs_2_, f32[16,1664]{1,0:T(8,128)S(1)} %collective-permute-done.5.refs_3_), custom_call_target="tpu_custom_call" | custom-call | tf_op jit(solution)/shard_map/pallas_call | solution.py:165
  (5 shorter events, 0.1 us)
Async XLA Ops:
  0.0 0.7 %copy-start.1 = (s32[64,2]{0,1:T(2,128)S(1)}, s32[64,2]{0,1:T(2,128)}, u32[]{:S(2)}) copy-start(s32[64,2]{0,1:T(2,128)} %param.7) | copy-start | bytes 1540
  0.0 0.7 %copy-start.2 = (s32[256]{0:T(256)S(1)}, s32[256]{0:T(256)}, u32[]{:S(2)}) copy-start(s32[256]{0:T(256)} %param.9) | copy-start | bytes 3076
  0.0 0.9 %copy-start = (bf16[4096,16]{0,1:T(8,128)(2,1)S(1)}, bf16[4096,16]{0,1:T(8,128)(2,1)}, u32[]{:S(2)}) copy-start(bf16[4096,16]{0,1:T(8,128)(2,1)} %param.6) | copy-start | bytes 393220
  0.0 12.6 %copy-start.3 = (s32[24]{0:T(128)S(1)}, s32[24]{0:T(128)}, u32[]{:S(2)}) copy-start(s32[24]{0:T(128)} %param.8) | copy-start | bytes 292
  7.1 2.4 %collective-permute-start = (f32[128,1536]{1,0:T(8,128)S(1)}, f32[128,1536]{1,0:T(8,128)S(1)}, u32[]{:S(2)}, u32[]{:S(2)}) collective-permute-start(f32[128,1536]{1,0:T(8,128)S(1)} %get-tuple-element.16), channel_id=1, source_target_pairs={{0,1},{1,0},{2,3},{3,2},{4,5},{5,4},{6,7},{7,6},{8,9},{9,8},{10,11... | collective-permute-start | bytes 2359304 | tf_op jit(solution)/shard_map/ppermute | solution.py:223
  9.6 8.6 %collective-permute-start.2 = (f32[32,1536]{1,0:T(8,128)S(1)}, f32[32,1536]{1,0:T(8,128)S(1)}, u32[]{:S(2)}, u32[]{:S(2)}) collective-permute-start(f32[32,1536]{1,0:T(8,128)S(1)} %get-tuple-element.20), channel_id=1, source_target_pairs={{0,2},{1,3},{2,0},{3,1},{4,6},{5,7},{6,4},{7,5},{8,10},{9,11},{10,... | collective-permute-start | bytes 589832 | tf_op jit(solution)/shard_map/ppermute | solution.py:223
  12.6 10.2 %collective-permute-start.1 = (f32[32,1536]{1,0:T(8,128)S(1)}, f32[32,1536]{1,0:T(8,128)S(1)}, u32[]{:S(2)}, u32[]{:S(2)}) collective-permute-start(f32[32,1536]{1,0:T(8,128)S(1)} %get-tuple-element.19), channel_id=1, source_target_pairs={{0,2},{1,3},{2,0},{3,1},{4,6},{5,7},{6,4},{7,5},{8,10},{9,11},{10,... | collective-permute-start | bytes 589832 | tf_op jit(solution)/shard_map/ppermute | solution.py:223
  18.2 10.6 %collective-permute-start.3 = (f32[16,1664]{1,0:T(8,128)S(1)}, f32[16,1664]{1,0:T(8,128)S(1)}, u32[]{:S(2)}, u32[]{:S(2)}) collective-permute-start(f32[16,1664]{1,0:T(8,128)S(1)} %get-tuple-element.21.earlier), channel_id=1, source_target_pairs={{0,8},{4,12},{8,0},{12,4},{1,9},{5,13},{9,1},{13,5},{2,10},{6,14},... | collective-permute-start | bytes 319496 | tf_op jit(solution)/shard_map/ppermute | solution.py:223
  21.4 7.4 %collective-permute-start.4 = (f32[16,1664]{1,0:T(8,128)S(1)}, f32[16,1664]{1,0:T(8,128)S(1)}, u32[]{:S(2)}, u32[]{:S(2)}) collective-permute-start(f32[16,1664]{1,0:T(8,128)S(1)} %get-tuple-element.23), channel_id=1, source_target_pairs={{0,12},{4,8},{8,4},{12,0},{1,13},{5,9},{9,5},{13,1},{2,14},{6,10},... | collective-permute-start | bytes 319496 | tf_op jit(solution)/shard_map/ppermute | solution.py:223
  22.8 6.5 %collective-permute-start.5 = (f32[16,1664]{1,0:T(8,128)S(1)}, f32[16,1664]{1,0:T(8,128)S(1)}, u32[]{:S(2)}, u32[]{:S(2)}) collective-permute-start(f32[16,1664]{1,0:T(8,128)S(1)} %get-tuple-element.24), channel_id=1, source_target_pairs={{0,4},{4,0},{8,12},{12,8},{1,5},{5,1},{9,13},{13,9},{2,6},{6,2},{1... | collective-permute-start | bytes 319496 | tf_op jit(solution)/shard_map/ppermute | solution.py:223

commit v4 on v3

--- a/solution.py
+++ b/solution.py
@@ -24,11 +24,13 @@
     rows_each = NIJ // (pairs * ranges)
     place = lax.broadcasted_iota(jnp.int32, (SHELL, NIJ), 1)
     inner = place % rows_each
-    far_pair = (place // rows_each) % pairs
-    order = place // (rows_each * pairs)
-    far_range = jnp.zeros_like(order)
-    for bit in range(bits(ranges)):
-        far_range = far_range + (((order >> (bits(ranges) - 1 - bit)) & 1) << bit)
+    block = place // rows_each
+    low = block % (pairs // 2)
+    block = block // (pairs // 2)
+    far_range = block // ranges
+    for bit in range(1, bits(ranges)):
+        far_range = far_range + (((block >> (bits(ranges) - 1 - bit)) & 1) << bit)
+    far_pair = low + ((block // (ranges // 2)) % 2) * (pairs // 2)
     target = ((far_pair ^ me_pair) * ranges + (far_range ^ me_range)) * rows_each + inner
     row = lax.broadcasted_iota(jnp.int32, (NIJ, NIJ), 0)
     moved[...] = (row == target[0:1, :]).astype(jnp.bfloat16)
@@ -45,9 +47,10 @@
 
 
 def half_rows_kernel(
-    shells_at, owner_at, coef_at, moved, integrals, keep, send, shells, owner, coef,
+    shells_at, owner, coef, moved, integrals, keep_near, keep_far, send_near, send_far, shells,
     table, lam, sig, cols, held, small, sems,
 ):
+    outs = keep_near, keep_far, send_near, send_far
     steps = sems.shape[0]
     depth = held.shape[1] // steps
     kets = cols.shape[0] // BLOCK_PAIRS
@@ -56,19 +59,12 @@
         here = pl.ds(step * depth, depth)
         return pltpu.make_async_copy(integrals.at[:, here], held.at[:, here], sems.at[step])
 
-    tables = [
-        pltpu.make_async_copy(shells_at, shells, small.at[0]),
-        pltpu.make_async_copy(owner_at, owner, small.at[1]),
-        pltpu.make_async_copy(coef_at, coef, small.at[2]),
-    ]
-    for copy in tables:
-        copy.start()
+    copy = pltpu.make_async_copy(shells_at, shells, small)
+    copy.start()
     for step in range(steps):
         fetch(step).start()
 
     orbital = lax.broadcasted_iota(jnp.int32, (NOCC, NIJ), 0)
-    for copy in tables:
-        copy.wait()
     picks = jnp.concatenate(
         [
             (owner[...] // NOCC == orbital).astype(jnp.bfloat16),
@@ -79,6 +75,7 @@
     picks = jnp.dot(picks, moved[...], preferred_element_type=jnp.float32).astype(jnp.bfloat16)
 
     table[...] = coef[...].astype(jnp.float32).T
+    copy.wait()
 
     for k in range(kets):
         here = pl.ds(k * SHELL, SHELL)
@@ -104,32 +101,30 @@
             cols[here, :], held[:, here], (((0,), (1,)), ((), ())),
             preferred_element_type=jnp.float32,
         )
-        for at, out in enumerate((keep, send)):
-            half = part[at * (NIJ // 2) : (at + 1) * (NIJ // 2)]
-            out[...] = half if step == 0 else out[...] + half
+        for at, out in enumerate(outs):
+            rows = part[at * (NIJ // 4) : (at + 1) * (NIJ // 4)]
+            out[...] = rows if step == 0 else out[...] + rows
 
 
 def half_rows(integrals, coefficients, ket_shells, pair_owner, pairs, ranges):
     rows, depth = integrals.shape
     kets = ket_shells.shape[0]
-    half = jax.ShapeDtypeStruct((NIJ // 2, rows), jnp.float32)
-    vmem = pl.BlockSpec(memory_space=pltpu.VMEM)
+    part = jax.ShapeDtypeStruct((NIJ // 4, rows), jnp.float32)
+    vmem = pl.BlockSpec(memory_space=pltpu.VMEM)
+    hbm = pl.BlockSpec(memory_space=pl.ANY)
     return pl.pallas_call(
         half_rows_kernel,
-        out_shape=(half, half),
-        in_specs=[pl.BlockSpec(memory_space=pl.ANY)] * 3
-        + [vmem, pl.BlockSpec(memory_space=pl.ANY)],
-        out_specs=(vmem, vmem),
+        out_shape=[part] * 4,
+        in_specs=[hbm, vmem, vmem, vmem, hbm],
+        out_specs=[vmem] * 4,
         scratch_shapes=[
             pltpu.SMEM((2, kets), jnp.int32),
-            pltpu.VMEM((1, NIJ), jnp.int32),
-            pltpu.VMEM((NOCC, coefficients.shape[0]), jnp.bfloat16),
             pltpu.VMEM((coefficients.shape[0], NOCC), jnp.float32),
             pltpu.VMEM((kets * SHELL, NIJ), jnp.float32),
             pltpu.VMEM((kets * SHELL, NIJ), jnp.float32),
             pltpu.VMEM((depth, NIJ), jnp.bfloat16),
             pltpu.VMEM((rows, depth), jnp.bfloat16),
-            pltpu.SemaphoreType.DMA((3,)),
+            pltpu.SemaphoreType.DMA,
             pltpu.SemaphoreType.DMA((STEPS,)),
         ],
         compiler_params=pltpu.CompilerParams(vmem_limit_bytes=52 * MIB),
@@ -184,7 +179,7 @@
         out[pl.ds(place * size, size), :] = mine[here, :] + theirs[here, :]
 
 
-def summed(mine, theirs, earlier, spans):
+def summed(mine, theirs, earlier, spans, cost):
     vmem = pl.BlockSpec(memory_space=pltpu.VMEM)
     rows = sum(size for _, size in spans) // 2
     half = jax.ShapeDtypeStruct((rows, mine.shape[1]), jnp.float32)
@@ -193,28 +188,30 @@
         out_shape=[half] * 2,
         in_specs=[vmem] * 2 + [pl.BlockSpec(memory_space=pl.ANY)],
         out_specs=[vmem] * 2,
+        cost_estimate=pl.CostEstimate(flops=cost, bytes_accessed=0, transcendentals=0),
         compiler_params=pltpu.CompilerParams(vmem_limit_bytes=8 * MIB),
     )(mine, theirs, earlier)
 
 
-def merge_kernel(count, mine_from, mine, theirs, ids, earlier, *outs):
+def merge_kernel(count, mine, theirs, ids, earlier, *outs):
     width = mine.shape[1]
     rows = outs[0].shape[0]
     for d in range(count):
         here = pl.ds(d * rows, rows)
-        outs[d][:, :width] = mine[pl.ds(mine_from + d * rows, rows), :] + theirs[here, :]
+        outs[d][:, :width] = mine[here, :] + theirs[here, :]
         outs[d][:, width:] = jnp.broadcast_to(ids[...], (rows, LANES))
 
 
-def merged(mine, mine_from, theirs, ids, earlier, count):
+def merged(mine, theirs, ids, earlier, count, cost):
     vmem = pl.BlockSpec(memory_space=pltpu.VMEM)
     rows = theirs.shape[0] // count
     one = jax.ShapeDtypeStruct((rows, mine.shape[1] + LANES), jnp.float32)
     return pl.pallas_call(
-        functools.partial(merge_kernel, count, mine_from),
+        functools.partial(merge_kernel, count),
         out_shape=[one] * count,
         in_specs=[vmem] * 3 + [pl.BlockSpec(memory_space=pl.ANY)],
         out_specs=[vmem] * count,
+        cost_estimate=pl.CostEstimate(flops=cost, bytes_accessed=0, transcendentals=0),
         compiler_params=pltpu.CompilerParams(vmem_limit_bytes=8 * MIB),
     )(mine, theirs, ids, earlier)
 
@@ -225,30 +222,36 @@
 
 def local(pairs, ranges, integrals, coefficients, ket_shells, block_ids, pair_owner):
     slots = block_ids.shape[0]
-    keep, send = half_rows(integrals, coefficients, ket_shells, pair_owner, pairs, ranges)
-    across = swap(send, "rng", ranges, 1)
+    near, far, send_near, send_far = half_rows(
+        integrals, coefficients, ket_shells, pair_owner, pairs, ranges
+    )
+    far = far, swap(send_far, "rng", ranges, 1)
+    near = near, swap(send_near, "rng", ranges, 1)
     each = NIJ // (pairs * ranges)
     numbers = jnp.pad(block_ids.astype(jnp.float32), (0, LANES - slots)).reshape(1, LANES)
-    step = max(pairs // 2, 1)
-    size = step * each
+    step = pairs // 2
+    some = max(step // 2, 1)
+    groups = [(far, at, step, some) for at in range(0, step, some)] + [(near, 0, 0, step)]
     halves = []
-    earlier = across
-    for first in range(0, pairs, step)[::-1]:
-        spans = tuple(((o * pairs + first) * each, size) for o in range(ranges // 2))
-        lower, upper = summed(keep, across, earlier, spans)
-        halves.append((first, lower, upper))
+    earlier = far[1]
+    for sums, at, base, count in groups:
+        spans = tuple(
+            ((o * step + at) * each, count * each) for o in range(ranges // 2)
+        )
+        lower, upper = summed(*sums, earlier, spans, 10**6 if base else 5 * 10**8)
+        halves.append((base + at, count, lower, upper))
         earlier = lower
     pieces = [None] * pairs
     earlier = numbers
-    for first, lower, upper in halves:
+    for first, count, lower, upper in halves:
         for bit in range(1, bits(ranges)):
             other = swap(upper, "rng", ranges, 1 << bit)
             if bit < bits(ranges) - 1:
                 lower = lower + other
                 lower, upper = jnp.split(lower, 2)
-        parts = merged(lower, 0, other, numbers, earlier, step)
+        parts = merged(lower, other, numbers, earlier, count, 10**9 if first == step else 10**10)
         earlier = parts[0]
-        for at in range(step):
+        for at in range(count):
             d = first + at
             pieces[d] = swap(parts[at], "pair", pairs, d) if d else parts[at]
     pieces = pieces[:1] + pieces[step:] + pieces[1:step]

time: 31.5 us -> 29.7 us (0.943)
  waiting for transfers between devices: 12.9 us -> 6.9 us
  starting transfers between devices: 9.11 us -> 13.4 us
    ppermute x6 -> x8, waiting for transfers between devices: 12.9 us -> 6.9 us  [swap(): return lax.ppermute(value, axis, [(i, i ^ far) for i in range(size)])]
    ppermute x6 -> x8, starting transfers between devices: 9.11 us -> 13.4 us  [swap(): return lax.ppermute(value, axis, [(i, i ^ far) for i in range(size)])]
    pallas_call x3 -> x4, Pallas kernels: 6.21 us -> 6.26 us  [the longest x1 6.21 us: half_rows(): pl.pallas_call(half_rows_kernel, out_shape=[part] * 4, in_specs=[hbm, vme...]
  transfers between devices with their start and end apart: 6 -> 8, of which waited for: 4 -> 4; matrix products, arithmetic and copies ran while one was open for 0% -> 0% of each run, Pallas kernels for 0% -> 0%
where the time goes in v4:
time: 29.7 us; the launch traced here: 29.6 us
  starting transfers between devices  13.4 us (45%)
  Pallas kernels  8.4 us (28%)
  waiting for transfers between devices  6.9 us (23%)
  local copies, waits for them, and re-layouts  0.88 us (3%)
    ppermute x8, starting transfers between devices, swap(): return lax.ppermute(value, axis, [(i, i ^ far) for i in range(size)])  13.4 us
    ppermute x8, waiting for transfers between devices, swap(): return lax.ppermute(value, axis, [(i, i ^ far) for i in range(size)])  6.9 us
    pallas_call x1, Pallas kernels, half_rows(): pl.pallas_call(half_rows_kernel, out_shape=[part] * 4, in_specs=[hbm, vme...  6.21 us
    pallas_call x1, Pallas kernels, placed_rows(): pl.pallas_call(functools.partial(place_kernel, slots), out_shape=jax.Shap...  2.01 us
    unnamed x8, local copies, waits for them, and re-layouts  0.87 us
  transfers between devices with their start and end apart: 8, of which 4 were waited for; matrix products, arithmetic and copies ran while one was open for 0% of the time, Pallas kernels for 0%

profile of v4, /device:TPU:0, one launch (start us, length us, event | category | flops | bytes accessed | tf_op | source)
XLA Modules:
  0.0 29.6 jit_solution(6099967727888158707)
XLA Ops:
  0.0 0.0 copy-start.1
  0.0 0.0 copy-start.2
  0.0 0.0 copy-start
  0.0 0.1 shard_map.55.moved
  0.1 0.0 copy-start.3
  0.1 0.6 %copy-done.1 = s32[64,2]{0,1:T(2,128)S(1)} copy-done((s32[64,2]{0,1:T(2,128)S(1)}, s32[64,2]{0,1:T(2,128)}, u32[]{:S(2)}) %copy-start.1) | copy-done | bytes 536
  0.7 0.0 copy-done.2
  0.7 0.2 copy-done
  0.9 6.2 %shard_map.56 = (f32[64,1536]{1,0:T(8,128)S(1)}, f32[64,1536]{1,0:T(8,128)S(1)}, f32[64,1536]{1,0:T(8,128)S(1)}, f32[64,1536]{1,0:T(8,128)S(1)}) custom-call(s32[2,64]{1,0:T(2,128)S(1)} %bitcast.6, s32[1,256]{1,0:T(1,128)S(1)} %bitcast.7, bf16[16,4096]{1,0:T(8,128)(2,1)S(1)} %bitcast.5, bf16[256,256]{1,0:T(8,128)(2,1)S(1)} %shard_map.55.moved, ...), custom_call_target="tpu_custom_call" | custom-call | tf_op jit(solution)/shard_map/pallas_call | solution.py:115
  7.2 0.5 %collective-permute-start.1 = (f32[64,1536]{1,0:T(8,128)S(1)}, f32[64,1536]{1,0:T(8,128)S(1)}, u32[]{:S(2)}, u32[]{:S(2)}) collective-permute-start(f32[64,1536]{1,0:T(8,128)S(1)} %get-tuple-element.20), channel_id=1, source_target_pairs={{0,1},{1,0},{2,3},{3,2},{4,5},{5,4},{6,7},{7,6},{8,9},{9,8},{10,11... | collective-permute-start | bytes 1179656 | tf_op jit(solution)/shard_map/ppermute | solution.py:220
  7.7 0.1 collective-permute-start
  7.7 0.0 copy-done.3
  7.7 1.3 %collective-permute-done.1.theirs.earlier = f32[64,1536]{1,0:T(8,128)S(1)} collective-permute-done((f32[64,1536]{1,0:T(8,128)S(1)}, f32[64,1536]{1,0:T(8,128)S(1)}, u32[]{:S(2)}, u32[]{:S(2)}) %collective-permute-start.1) | collective-permute-done | bytes 393248 | tf_op jit(solution)/shard_map/ppermute | solution.py:220
  9.0 2.9 %collective-permute-start.4 = (f32[16,1536]{1,0:T(8,128)S(1)}, f32[16,1536]{1,0:T(8,128)S(1)}, u32[]{:S(2)}, u32[]{:S(2)}) collective-permute-start(f32[16,1536]{1,0:T(8,128)S(1)} %get-tuple-element.26), channel_id=1, source_target_pairs={{0,2},{1,3},{2,0},{3,1},{4,6},{5,7},{6,4},{7,5},{8,10},{9,11},{10,... | collective-permute-start | bytes 294920 | tf_op jit(solution)/shard_map/ppermute | solution.py:220
  12.0 0.1 collective-permute-start.3
  12.1 0.0 collective-permute-done.theirs
  12.1 2.1 %collective-permute-start.2 = (f32[32,1536]{1,0:T(8,128)S(1)}, f32[32,1536]{1,0:T(8,128)S(1)}, u32[]{:S(2)}, u32[]{:S(2)}) collective-permute-start(f32[32,1536]{1,0:T(8,128)S(1)} %get-tuple-element.24), channel_id=1, source_target_pairs={{0,2},{1,3},{2,0},{3,1},{4,6},{5,7},{6,4},{7,5},{8,10},{9,11},{10,... | collective-permute-start | bytes 589832 | tf_op jit(solution)/shard_map/ppermute | solution.py:220
  14.2 1.3 %collective-permute-done.4.theirs = f32[16,1536]{1,0:T(8,128)S(1)} collective-permute-done((f32[16,1536]{1,0:T(8,128)S(1)}, f32[16,1536]{1,0:T(8,128)S(1)}, u32[]{:S(2)}, u32[]{:S(2)}) %collective-permute-start.4) | collective-permute-done | bytes 98336 | tf_op jit(solution)/shard_map/ppermute | solution.py:220
  15.6 3.2 %collective-permute-start.5 = (f32[16,1664]{1,0:T(8,128)S(1)}, f32[16,1664]{1,0:T(8,128)S(1)}, u32[]{:S(2)}, u32[]{:S(2)}) collective-permute-start(f32[16,1664]{1,0:T(8,128)S(1)} %shard_map.60.earlier), channel_id=1, source_target_pairs={{0,8},{4,12},{8,0},{12,4},{1,9},{5,13},{9,1},{13,5},{2,10},{6,14},... | collective-permute-start | bytes 319496 | tf_op jit(solution)/shard_map/ppermute | solution.py:220
  18.8 0.0 collective-permute-done.3.theirs
  18.8 3.1 %collective-permute-start.6 = (f32[16,1664]{1,0:T(8,128)S(1)}, f32[16,1664]{1,0:T(8,128)S(1)}, u32[]{:S(2)}, u32[]{:S(2)}) collective-permute-start(f32[16,1664]{1,0:T(8,128)S(1)} %shard_map.61.earlier), channel_id=1, source_target_pairs={{0,12},{4,8},{8,4},{12,0},{1,13},{5,9},{9,5},{13,1},{2,14},{6,10},... | collective-permute-start | bytes 319496 | tf_op jit(solution)/shard_map/ppermute | solution.py:220
  21.9 0.0 collective-permute-done.2.theirs
  21.9 1.4 %collective-permute-start.7 = (f32[16,1664]{1,0:T(8,128)S(1)}, f32[16,1664]{1,0:T(8,128)S(1)}, u32[]{:S(2)}, u32[]{:S(2)}) collective-permute-start(f32[16,1664]{1,0:T(8,128)S(1)} %get-tuple-element.28), channel_id=1, source_target_pairs={{0,4},{4,0},{8,12},{12,8},{1,5},{5,1},{9,13},{13,9},{2,6},{6,2},{1... | collective-permute-start | bytes 319496 | tf_op jit(solution)/shard_map/ppermute | solution.py:220
  23.3 2.8 %collective-permute-done.5.refs_1_ = f32[16,1664]{1,0:T(8,128)S(1)} collective-permute-done((f32[16,1664]{1,0:T(8,128)S(1)}, f32[16,1664]{1,0:T(8,128)S(1)}, u32[]{:S(2)}, u32[]{:S(2)}) %collective-permute-start.5) | collective-permute-done | bytes 106528 | tf_op jit(solution)/shard_map/ppermute | solution.py:220
  26.1 0.0 collective-permute-done.6.refs_2_
  26.1 1.4 %collective-permute-done.7.refs_3_ = f32[16,1664]{1,0:T(8,128)S(1)} collective-permute-done((f32[16,1664]{1,0:T(8,128)S(1)}, f32[16,1664]{1,0:T(8,128)S(1)}, u32[]{:S(2)}, u32[]{:S(2)}) %collective-permute-start.7) | collective-permute-done | bytes 106528 | tf_op jit(solution)/shard_map/ppermute | solution.py:220
  27.6 2.0 %shard_map.63 = f32[16,3072]{1,0:T(8,128)} custom-call(f32[16,1664]{1,0:T(8,128)S(1)} %get-tuple-element.27.refs_0_, f32[16,1664]{1,0:T(8,128)S(1)} %collective-permute-done.5.refs_1_, f32[16,1664]{1,0:T(8,128)S(1)} %collective-permute-done.6.refs_2_, f32[16,1664]{1,0:T(8,128)S(1)} %collective-permute-done.7.refs_3_), custom_call_target="tpu_custom_call" | custom-call | tf_op jit(solution)/shard_map/pallas_call | solution.py:160
  (8 shorter events, 0.1 us)
Async XLA Ops:
  0.0 0.7 %copy-start.1 = (s32[64,2]{0,1:T(2,128)S(1)}, s32[64,2]{0,1:T(2,128)}, u32[]{:S(2)}) copy-start(s32[64,2]{0,1:T(2,128)} %param.7) | copy-start | bytes 1540
  0.0 0.7 %copy-start.2 = (s32[256]{0:T(256)S(1)}, s32[256]{0:T(256)}, u32[]{:S(2)}) copy-start(s32[256]{0:T(256)} %param.9) | copy-start | bytes 3076
  0.0 0.9 %copy-start = (bf16[4096,16]{0,1:T(8,128)(2,1)S(1)}, bf16[4096,16]{0,1:T(8,128)(2,1)}, u32[]{:S(2)}) copy-start(bf16[4096,16]{0,1:T(8,128)(2,1)} %param.6) | copy-start | bytes 393220
  0.1 7.7 %copy-start.3 = (s32[24]{0:T(128)S(1)}, s32[24]{0:T(128)}, u32[]{:S(2)}) copy-start(s32[24]{0:T(128)} %param.8) | copy-start | bytes 292
  7.2 1.9 %collective-permute-start.1 = (f32[64,1536]{1,0:T(8,128)S(1)}, f32[64,1536]{1,0:T(8,128)S(1)}, u32[]{:S(2)}, u32[]{:S(2)}) collective-permute-start(f32[64,1536]{1,0:T(8,128)S(1)} %get-tuple-element.20), channel_id=1, source_target_pairs={{0,1},{1,0},{2,3},{3,2},{4,5},{5,4},{6,7},{7,6},{8,9},{9,8},{10,11... | collective-permute-start | bytes 1179656 | tf_op jit(solution)/shard_map/ppermute | solution.py:220
  7.7 4.4 %collective-permute-start = (f32[64,1536]{1,0:T(8,128)S(1)}, f32[64,1536]{1,0:T(8,128)S(1)}, u32[]{:S(2)}, u32[]{:S(2)}) collective-permute-start(f32[64,1536]{1,0:T(8,128)S(1)} %get-tuple-element.18), channel_id=1, source_target_pairs={{0,1},{1,0},{2,3},{3,2},{4,5},{5,4},{6,7},{7,6},{8,9},{9,8},{10,11... | collective-permute-start | bytes 1179656 | tf_op jit(solution)/shard_map/ppermute | solution.py:220
  9.0 6.5 %collective-permute-start.4 = (f32[16,1536]{1,0:T(8,128)S(1)}, f32[16,1536]{1,0:T(8,128)S(1)}, u32[]{:S(2)}, u32[]{:S(2)}) collective-permute-start(f32[16,1536]{1,0:T(8,128)S(1)} %get-tuple-element.26), channel_id=1, source_target_pairs={{0,2},{1,3},{2,0},{3,1},{4,6},{5,7},{6,4},{7,5},{8,10},{9,11},{10,... | collective-permute-start | bytes 294920 | tf_op jit(solution)/shard_map/ppermute | solution.py:220
  12.0 6.8 %collective-permute-start.3 = (f32[16,1536]{1,0:T(8,128)S(1)}, f32[16,1536]{1,0:T(8,128)S(1)}, u32[]{:S(2)}, u32[]{:S(2)}) collective-permute-start(f32[16,1536]{1,0:T(8,128)S(1)} %get-tuple-element.25), channel_id=1, source_target_pairs={{0,2},{1,3},{2,0},{3,1},{4,6},{5,7},{6,4},{7,5},{8,10},{9,11},{10,... | collective-permute-start | bytes 294920 | tf_op jit(solution)/shard_map/ppermute | solution.py:220
  12.1 9.8 %collective-permute-start.2 = (f32[32,1536]{1,0:T(8,128)S(1)}, f32[32,1536]{1,0:T(8,128)S(1)}, u32[]{:S(2)}, u32[]{:S(2)}) collective-permute-start(f32[32,1536]{1,0:T(8,128)S(1)} %get-tuple-element.24), channel_id=1, source_target_pairs={{0,2},{1,3},{2,0},{3,1},{4,6},{5,7},{6,4},{7,5},{8,10},{9,11},{10,... | collective-permute-start | bytes 589832 | tf_op jit(solution)/shard_map/ppermute | solution.py:220
  15.6 10.6 %collective-permute-start.5 = (f32[16,1664]{1,0:T(8,128)S(1)}, f32[16,1664]{1,0:T(8,128)S(1)}, u32[]{:S(2)}, u32[]{:S(2)}) collective-permute-start(f32[16,1664]{1,0:T(8,128)S(1)} %shard_map.60.earlier), channel_id=1, source_target_pairs={{0,8},{4,12},{8,0},{12,4},{1,9},{5,13},{9,1},{13,5},{2,10},{6,14},... | collective-permute-start | bytes 319496 | tf_op jit(solution)/shard_map/ppermute | solution.py:220
  18.8 7.3 %collective-permute-start.6 = (f32[16,1664]{1,0:T(8,128)S(1)}, f32[16,1664]{1,0:T(8,128)S(1)}, u32[]{:S(2)}, u32[]{:S(2)}) collective-permute-start(f32[16,1664]{1,0:T(8,128)S(1)} %shard_map.61.earlier), channel_id=1, source_target_pairs={{0,12},{4,8},{8,4},{12,0},{1,13},{5,9},{9,5},{13,1},{2,14},{6,10},... | collective-permute-start | bytes 319496 | tf_op jit(solution)/shard_map/ppermute | solution.py:220
  21.9 5.7 %collective-permute-start.7 = (f32[16,1664]{1,0:T(8,128)S(1)}, f32[16,1664]{1,0:T(8,128)S(1)}, u32[]{:S(2)}, u32[]{:S(2)}) collective-permute-start(f32[16,1664]{1,0:T(8,128)S(1)} %get-tuple-element.28), channel_id=1, source_target_pairs={{0,4},{4,0},{8,12},{12,8},{1,5},{5,1},{9,13},{13,9},{2,6},{6,2},{1... | collective-permute-start | bytes 319496 | tf_op jit(solution)/shard_map/ppermute | solution.py:220

commit v5 on v4

v5 whole, which is shorter than its diff:
```python
import functools
import jax
import jax.numpy as jnp
from jax import lax
from jax.experimental import pallas as pl
from jax.experimental.pallas import tpu as pltpu
from jax.sharding import PartitionSpec as P

SHELL = 8
BLOCK_PAIRS = 64
NOCC = 16
NIJ = 256
LANES = 128
CHUNKS = 4, 4, 4, 4
MIB = 1 << 20


def bits(size):
    return size.bit_length() - 1


def order_kernel(pairs, ranges, moved):
    me_pair, me_range = lax.axis_index("pair"), lax.axis_index("rng")
    rows_each = NIJ // (pairs * ranges)
    place = lax.broadcasted_iota(jnp.int32, (SHELL, NIJ), 1)
    inner = place % rows_each
    block = place // rows_each
    step, some, chips = pairs // 2, max(pairs // 4, 1), ranges // 2
    core = block // (pairs * chips)
    high = (block // (step * chips)) % 2
    block = block % (step * chips)
    far = high == 1
    low = jnp.where(far, (block // (some * chips)) * some + block % some, block % step)
    order = jnp.where(far, (block // some) % chips, block // step)
    far_range = core
    for bit in range(1, bits(ranges)):
        far_range = far_range + (((order >> (bits(ranges) - 1 - bit)) & 1) << bit)
    far_pair = low + high * step
    target = ((far_pair ^ me_pair) * ranges + (far_range ^ me_range)) * rows_each + inner
    row = lax.broadcasted_iota(jnp.int32, (NIJ, NIJ), 0)
    moved[...] = (row == target[0:1, :]).astype(jnp.bfloat16)


def order_of(pairs, ranges):
    return pl.pallas_call(
        functools.partial(order_kernel, pairs, ranges),
        out_shape=jax.ShapeDtypeStruct((NIJ, NIJ), jnp.bfloat16),
        out_specs=pl.BlockSpec(memory_space=pltpu.VMEM),
        compiler_params=pltpu.CompilerParams(vmem_limit_bytes=8 * MIB),
        cost_estimate=pl.CostEstimate(flops=10**10, bytes_accessed=NIJ * NIJ * 2, transcendentals=0),
    )()


def half_rows_kernel(spans, shells_at, owner, coef, moved, integrals, *refs):
    outs, (shells, table, lam, sig, cols, held, small, sems) = refs[:-8], refs[-8:]
    steps = len(spans)

    def fetch(step):
        here = pl.ds(*spans[step])
        return pltpu.make_async_copy(integrals.at[:, here], held.at[:, here], sems.at[step])

    copy = pltpu.make_async_copy(shells_at, shells, small)
    copy.start()
    for step in range(steps):
        fetch(step).start()

    orbital = lax.broadcasted_iota(jnp.int32, (NOCC, NIJ), 0)
    picks = jnp.concatenate(
        [
            (owner[...] // NOCC == orbital).astype(jnp.bfloat16),
            (owner[...] % NOCC == orbital).astype(jnp.bfloat16),
        ],
        axis=0,
    )
    picks = jnp.dot(picks, moved[...], preferred_element_type=jnp.float32).astype(jnp.bfloat16)

    table[...] = coef[...].astype(jnp.float32).T
    copy.wait()

    for k in range(lam.shape[0] // SHELL):
        here = pl.ds(k * SHELL, SHELL)
        lam[here, :NOCC] = table[pl.ds(pl.multiple_of(shells[0, k] * SHELL, SHELL), SHELL), :]
        sig[here, :NOCC] = table[pl.ds(pl.multiple_of(shells[1, k] * SHELL, SHELL), SHELL), :]
    lam[...] = jnp.dot(
        lam[:, :NOCC].astype(jnp.bfloat16), picks[:NOCC], preferred_element_type=jnp.float32
    )
    sig[...] = jnp.dot(
        sig[:, :NOCC].astype(jnp.bfloat16), picks[NOCC:], preferred_element_type=jnp.float32
    )
    for step in range(steps):
        start, size = spans[step]
        for k in range(start // BLOCK_PAIRS, (start + size) // BLOCK_PAIRS):
            here = pl.ds(k * SHELL, SHELL)
            both = lam[here, :][:, None, :] * sig[here, :][None, :, :]
            cols[pl.ds(k * BLOCK_PAIRS, BLOCK_PAIRS), :] = both.reshape(BLOCK_PAIRS, NIJ).astype(
                jnp.bfloat16
            )
        fetch(step).wait()
        part = lax.dot_general(
            cols[pl.ds(start, size), :], held[:, pl.ds(start, size)], (((0,), (1,)), ((), ())),
            preferred_element_type=jnp.float32,
        )
        at = 0
        for out in outs:
            rows = part[at : at + out.shape[0]]
            out[...] = rows if step == 0 else out[...] + rows
            at += out.shape[0]


def half_rows(integrals, coefficients, ket_shells, pair_owner, pairs, ranges, sizes):
    rows, depth = integrals.shape
    kets = ket_shells.shape[0]
    parts = [jax.ShapeDtypeStruct((size, rows), jnp.float32) for size in sizes * 2]
    ends = [sum(CHUNKS[:at]) * depth // 16 for at in range(len(CHUNKS) + 1)]
    spans = [(start, end - start) for start, end in zip(ends, ends[1:])]
    vmem = pl.BlockSpec(memory_space=pltpu.VMEM)
    hbm = pl.BlockSpec(memory_space=pl.ANY)
    return pl.pallas_call(
        functools.partial(half_rows_kernel, spans),
        out_shape=parts,
        in_specs=[hbm, vmem, vmem, vmem, hbm],
        out_specs=[vmem] * len(parts),
        scratch_shapes=[
            pltpu.SMEM((2, kets), jnp.int32),
            pltpu.VMEM((coefficients.shape[0], NOCC), jnp.float32),
            pltpu.VMEM((kets * SHELL, NIJ), jnp.float32),
            pltpu.VMEM((kets * SHELL, NIJ), jnp.float32),
            pltpu.VMEM((depth, NIJ), jnp.bfloat16),
            pltpu.VMEM((rows, depth), jnp.bfloat16),
            pltpu.SemaphoreType.DMA,
            pltpu.SemaphoreType.DMA((len(spans),)),
        ],
        compiler_params=pltpu.CompilerParams(vmem_limit_bytes=52 * MIB),
    )(ket_shells.T, pair_owner.reshape(1, NIJ), coefficients.T, order_of(pairs, ranges), integrals)


def place_kernel(slots, count, *refs):
    pieces, before = refs[:count], refs[count:-4]
    out, numbers, scalars, sem = refs[-4:]
    rows = out.shape[0]
    for d, piece in enumerate(pieces):
        numbers[pl.ds(d, 1), :] = piece[pl.ds(slots // 2 * rows, 1), :].astype(jnp.int32)
    copy = pltpu.make_async_copy(numbers, scalars, sem)
    copy.start()
    for done in before:
        out[...] = done[...]
    copy.wait()
    upper = lax.broadcasted_iota(jnp.int32, (out.shape[0], LANES), 1) // BLOCK_PAIRS
    for d, piece in enumerate(pieces):
        for tile in range(slots // 2):
            value = piece[pl.ds(tile * rows, rows), :]
            turned = pltpu.roll(value, BLOCK_PAIRS, 1)
            for side in range(2):
                block = scalars[d, 2 * tile + side]
                there = (jnp.maximum(block, 0) >> 1) * LANES
                pltpu.store(
                    out.at[:, pl.ds(pl.multiple_of(there, LANES), LANES)],
                    jnp.where((block & 1) == side, value, turned),
                    mask=upper == jnp.where(block >= 0, block & 1, 2),
                )


def placed_rows(pieces, before, slots, blocks):
    rows = pieces[0].shape[0] // (slots // 2)
    vmem = pl.BlockSpec(memory_space=pltpu.VMEM)
    return pl.pallas_call(
        functools.partial(place_kernel, slots, len(pieces)),
        out_shape=jax.ShapeDtypeStruct((rows, blocks * BLOCK_PAIRS), jnp.float32),
        in_specs=[vmem] * (len(pieces) + len(before)),
        out_specs=vmem,
        scratch_shapes=[
            pltpu.VMEM((len(pieces), LANES), jnp.int32),
            pltpu.SMEM((len(pieces), LANES), jnp.int32),
            pltpu.SemaphoreType.DMA,
        ],
        compiler_params=pltpu.CompilerParams(vmem_limit_bytes=8 * MIB),
    )(*pieces, *before)


def sum_kernel(mine, theirs, earlier, lower, upper):
    half = lower.shape[0]
    lower[...] = mine[:half] + theirs[:half]
    upper[...] = mine[half:] + theirs[half:]


def summed(mine, theirs, earlier, cost):
    vmem = pl.BlockSpec(memory_space=pltpu.VMEM)
    half = jax.ShapeDtypeStruct((mine.shape[0] // 2, mine.shape[1]), jnp.float32)
    return pl.pallas_call(
        sum_kernel,
        out_shape=[half] * 2,
        in_specs=[vmem] * 2 + [pl.BlockSpec(memory_space=pl.ANY)],
        out_specs=[vmem] * 2,
        cost_estimate=pl.CostEstimate(flops=cost, bytes_accessed=0, transcendentals=0),
        compiler_params=pltpu.CompilerParams(vmem_limit_bytes=8 * MIB),
    )(mine, theirs, earlier)


def merge_kernel(count, mine, theirs, ids, earlier, *outs):
    tiles = mine.shape[1] // LANES
    rows = mine.shape[0] // count
    for d in range(count):
        here = pl.ds(d * rows, rows)
        for tile in range(tiles):
            lanes = pl.ds(tile * LANES, LANES)
            outs[d][pl.ds(tile * rows, rows), :] = mine[here, lanes] + theirs[here, lanes]
        outs[d][pl.ds(tiles * rows, 1), :] = ids[...]


def merged(mine, theirs, ids, earlier, count, cost):
    vmem = pl.BlockSpec(memory_space=pltpu.VMEM)
    rows = theirs.shape[0] // count
    one = jax.ShapeDtypeStruct((rows * (mine.shape[1] // LANES) + 1, LANES), jnp.float32)
    return pl.pallas_call(
        functools.partial(merge_kernel, count),
        out_shape=[one] * count,
        in_specs=[vmem] * 3 + [pl.BlockSpec(memory_space=pl.ANY)],
        out_specs=[vmem] * count,
        cost_estimate=pl.CostEstimate(flops=cost, bytes_accessed=0, transcendentals=0),
        compiler_params=pltpu.CompilerParams(vmem_limit_bytes=8 * MIB),
    )(mine, theirs, ids, earlier)


def swap(value, axis, size, far):
    return lax.ppermute(value, axis, [(i, i ^ far) for i in range(size)])


def local(pairs, ranges, integrals, coefficients, ket_shells, block_ids, pair_owner):
    slots = block_ids.shape[0]
    each = NIJ // (pairs * ranges)
    step = pairs // 2
    some = max(step // 2, 1)
    groups = [(0, step)] + [(step + at, some) for at in range(0, step, some)]
    sizes = [count * each * (ranges // 2) for _, count in groups]
    parts = half_rows(integrals, coefficients, ket_shells, pair_owner, pairs, ranges, sizes)
    numbers = jnp.pad(block_ids.astype(jnp.float32), (0, LANES - slots)).reshape(1, LANES)
    groups = [
        (first, count, parts[at], parts[at + len(groups)])
        for at, (first, count) in enumerate(groups)
    ]
    groups = [
        (first, count, mine, swap(send, "rng", ranges, 1))
        for first, count, mine, send in groups[1:] + groups[:1]
    ]
    halves = []
    earlier = groups[0][3]
    for first, count, mine, theirs in groups:
        lower, upper = summed(mine, theirs, earlier, 5 * 10**8)
        halves.append((first, count, lower, upper))
        earlier = lower
    pieces = [None] * pairs
    earlier = numbers
    for first, count, lower, upper in halves:
        for bit in range(1, bits(ranges)):
            other = swap(upper, "rng", ranges, 1 << bit)
            if bit < bits(ranges) - 1:
                lower = lower + other
                lower, upper = jnp.split(lower, 2)
        parts = merged(lower, other, numbers, earlier, count, 10**9 if first == step else 2 * 10**9)
        earlier = parts[0]
        for at in range(count):
            d = first + at
            pieces[d] = swap(parts[at], "pair", pairs, d) if d else parts[at]
    blocks = slots * pairs // 2
    early = placed_rows(pieces[:1] + pieces[step:], [], slots, blocks)
    return placed_rows(pieces[1:step], [early], slots, blocks) if step > 1 else early


def solution(mesh):
    placed = (
        P(("grp", "pair"), "rng"),
        P("grp", None),
        P(("grp", "rng"), None),
        P(("grp", "pair")),
        P(),
    )
    return jax.shard_map(
        functools.partial(local, mesh.shape["pair"], mesh.shape["rng"]),
        mesh=mesh,
        in_specs=placed,
        out_specs=P(("grp", "pair", "rng"), None),
        check_vma=False,
    )
```

time: 29.7 us -> 28.5 us (0.960)
  waiting for transfers between devices: 6.9 us -> 5.01 us
  starting transfers between devices: 13.4 us -> 13.8 us
    ppermute x8 -> x9, waiting for transfers between devices: 6.9 us -> 5.01 us  [swap(): return lax.ppermute(value, axis, [(i, i ^ far) for i in range(size)])]
    ppermute x8 -> x9, starting transfers between devices: 13.4 us -> 13.8 us  [swap(): return lax.ppermute(value, axis, [(i, i ^ far) for i in range(size)])]
    pallas_call x5 -> x6, Pallas kernels: 8.3 us -> 8.51 us  [the longest x1 6.21 us: half_rows(): pl.pallas_call(functools.partial(half_rows_kernel, spans), out_shape=part...]
  transfers between devices with their start and end apart: 8 -> 9, of which waited for: 4 -> 5; matrix products, arithmetic and copies ran while one was open for 0% -> 0% of each run, Pallas kernels for 0% -> 4%
where the time goes in v5:
time: 28.5 us; the launch traced here: 28.4 us
  starting transfers between devices  13.8 us (48%)
  Pallas kernels  8.6 us (30%)
  waiting for transfers between devices  5.01 us (18%)
  local copies, waits for them, and re-layouts  0.88 us (3%)
    ppermute x9, starting transfers between devices, swap(): return lax.ppermute(value, axis, [(i, i ^ far) for i in range(size)])  13.8 us
    pallas_call x1, Pallas kernels, half_rows(): pl.pallas_call(functools.partial(half_rows_kernel, spans), out_shape=part...  6.21 us
    ppermute x9, waiting for transfers between devices, swap(): return lax.ppermute(value, axis, [(i, i ^ far) for i in range(size)])  5.01 us
    pallas_call x2, Pallas kernels, placed_rows(): pl.pallas_call(functools.partial(place_kernel, slots, len(pieces)), out_s...  2.21 us
    unnamed x8, local copies, waits for them, and re-layouts  0.88 us
  transfers between devices with their start and end apart: 9, of which 5 were waited for; matrix products, arithmetic and copies ran while one was open for 0% of the time, Pallas kernels for 4%

profile of v5, /device:TPU:0, one launch (start us, length us, event | category | flops | bytes accessed | tf_op | source)
XLA Modules:
  0.0 28.4 jit_solution(849633887400843958)
XLA Ops:
  0.0 0.0 copy-start.1
  0.0 0.0 copy-start.2
  0.0 0.0 copy-start
  0.1 0.0 copy-start.3
  0.1 0.6 %copy-done.1 = s32[64,2]{0,1:T(2,128)S(1)} copy-done((s32[64,2]{0,1:T(2,128)S(1)}, s32[64,2]{0,1:T(2,128)}, u32[]{:S(2)}) %copy-start.1) | copy-done | bytes 536
  0.7 0.0 copy-done.2
  0.7 0.2 copy-done
  0.9 6.2 %shard_map.56 = (f32[64,1536]{1,0:T(8,128)S(1)}, f32[32,1536]{1,0:T(8,128)S(1)}, f32[32,1536]{1,0:T(8,128)S(1)}, f32[64,1536]{1,0:T(8,128)S(1)}, f32[32,1536]{1,0:T(8,128)S(1)}, /*index=5*/f32[32,1536]{1,0:T(8,128)S(1)}) custom-call(s32[2,64]{1,0:T(2,128)S(1)} %bitcast.6, s32[1,256]{1,0:T(1,128)S(1)} %bitcast.7, bf16[16,4096]{1,0:T(8,128)(2,1)S(1)} %bitcast.5, ...), custom_call_target="tpu_custom_call" | custom-call | tf_op jit(solution)/shard_map/pallas_call | solution.py:118
  7.2 0.5 %collective-permute-start.2 = (f32[32,1536]{1,0:T(8,128)S(1)}, f32[32,1536]{1,0:T(8,128)S(1)}, u32[]{:S(2)}, u32[]{:S(2)}) collective-permute-start(f32[32,1536]{1,0:T(8,128)S(1)} %get-tuple-element.24), channel_id=1, source_target_pairs={{0,1},{1,0},{2,3},{3,2},{4,5},{5,4},{6,7},{7,6},{8,9},{9,8},{10,11... | collective-permute-start | bytes 589832 | tf_op jit(solution)/shard_map/ppermute | solution.py:225
  7.7 0.1 collective-permute-start
  7.7 0.4 %collective-permute-start.1 = (f32[32,1536]{1,0:T(8,128)S(1)}, f32[32,1536]{1,0:T(8,128)S(1)}, u32[]{:S(2)}, u32[]{:S(2)}) collective-permute-start(f32[32,1536]{1,0:T(8,128)S(1)} %get-tuple-element.22), channel_id=1, source_target_pairs={{0,1},{1,0},{2,3},{3,2},{4,5},{5,4},{6,7},{7,6},{8,9},{9,8},{10,11... | collective-permute-start | bytes 589832 | tf_op jit(solution)/shard_map/ppermute | solution.py:225
  8.2 0.0 copy-done.3
  8.2 0.6 %collective-permute-done.2.theirs.earlier = f32[32,1536]{1,0:T(8,128)S(1)} collective-permute-done((f32[32,1536]{1,0:T(8,128)S(1)}, f32[32,1536]{1,0:T(8,128)S(1)}, u32[]{:S(2)}, u32[]{:S(2)}) %collective-permute-start.2) | collective-permute-done | bytes 196640 | tf_op jit(solution)/shard_map/ppermute | solution.py:225
  8.8 2.9 %collective-permute-start.5 = (f32[16,1536]{1,0:T(8,128)S(1)}, f32[16,1536]{1,0:T(8,128)S(1)}, u32[]{:S(2)}, u32[]{:S(2)}) collective-permute-start(f32[16,1536]{1,0:T(8,128)S(1)} %get-tuple-element.30), channel_id=1, source_target_pairs={{0,2},{1,3},{2,0},{3,1},{4,6},{5,7},{6,4},{7,5},{8,10},{9,11},{10,... | collective-permute-start | bytes 294920 | tf_op jit(solution)/shard_map/ppermute | solution.py:225
  11.7 0.0 collective-permute-done.1.theirs
  11.7 0.8 %collective-permute-start.4 = (f32[16,1536]{1,0:T(8,128)S(1)}, f32[16,1536]{1,0:T(8,128)S(1)}, u32[]{:S(2)}, u32[]{:S(2)}) collective-permute-start(f32[16,1536]{1,0:T(8,128)S(1)} %get-tuple-element.29), channel_id=1, source_target_pairs={{0,2},{1,3},{2,0},{3,1},{4,6},{5,7},{6,4},{7,5},{8,10},{9,11},{10,... | collective-permute-start | bytes 294920 | tf_op jit(solution)/shard_map/ppermute | solution.py:225
  12.5 0.0 collective-permute-done.theirs
  12.6 1.3 %collective-permute-start.3 = (f32[32,1536]{1,0:T(8,128)S(1)}, f32[32,1536]{1,0:T(8,128)S(1)}, u32[]{:S(2)}, u32[]{:S(2)}) collective-permute-start(f32[32,1536]{1,0:T(8,128)S(1)} %get-tuple-element.28), channel_id=1, source_target_pairs={{0,2},{1,3},{2,0},{3,1},{4,6},{5,7},{6,4},{7,5},{8,10},{9,11},{10,... | collective-permute-start | bytes 589832 | tf_op jit(solution)/shard_map/ppermute | solution.py:225
  13.9 1.3 %collective-permute-done.5.theirs = f32[16,1536]{1,0:T(8,128)S(1)} collective-permute-done((f32[16,1536]{1,0:T(8,128)S(1)}, f32[16,1536]{1,0:T(8,128)S(1)}, u32[]{:S(2)}, u32[]{:S(2)}) %collective-permute-start.5) | collective-permute-done | bytes 98336 | tf_op jit(solution)/shard_map/ppermute | solution.py:225
  15.3 3.2 %collective-permute-start.7 = (f32[193,128]{1,0:T(8,128)S(1)}, f32[193,128]{1,0:T(8,128)S(1)}, u32[]{:S(2)}, u32[]{:S(2)}) collective-permute-start(f32[193,128]{1,0:T(8,128)S(1)} %shard_map.60.earlier), channel_id=1, source_target_pairs={{0,8},{4,12},{8,0},{12,4},{1,9},{5,13},{9,1},{13,5},{2,10},{6,14},... | collective-permute-start | bytes 296456 | tf_op jit(solution)/shard_map/ppermute | solution.py:225
  18.5 0.0 collective-permute-done.4.theirs
  18.5 3.1 %collective-permute-start.8 = (f32[193,128]{1,0:T(8,128)S(1)}, f32[193,128]{1,0:T(8,128)S(1)}, u32[]{:S(2)}, u32[]{:S(2)}) collective-permute-start(f32[193,128]{1,0:T(8,128)S(1)} %shard_map.61.earlier), channel_id=1, source_target_pairs={{0,12},{4,8},{8,4},{12,0},{1,13},{5,9},{9,5},{13,1},{2,14},{6,10},... | collective-permute-start | bytes 296456 | tf_op jit(solution)/shard_map/ppermute | solution.py:225
  21.6 0.0 collective-permute-done.3.theirs
  21.7 1.4 %collective-permute-start.6 = (f32[193,128]{1,0:T(8,128)S(1)}, f32[193,128]{1,0:T(8,128)S(1)}, u32[]{:S(2)}, u32[]{:S(2)}) collective-permute-start(f32[193,128]{1,0:T(8,128)S(1)} %get-tuple-element.31), channel_id=1, source_target_pairs={{0,4},{4,0},{8,12},{12,8},{1,5},{5,1},{9,13},{13,9},{2,6},{6,2},{1... | collective-permute-start | bytes 296456 | tf_op jit(solution)/shard_map/ppermute | solution.py:225
  23.0 2.2 %collective-permute-done.8.refs_2_ = f32[193,128]{1,0:T(8,128)S(1)} collective-permute-done((f32[193,128]{1,0:T(8,128)S(1)}, f32[193,128]{1,0:T(8,128)S(1)}, u32[]{:S(2)}, u32[]{:S(2)}) %collective-permute-start.8) | collective-permute-done | bytes 98848 | tf_op jit(solution)/shard_map/ppermute | solution.py:225
  25.2 0.2 collective-permute-done.7.refs_1_
  25.4 0.9 %shard_map.63.refs_1_ = f32[16,3072]{1,0:T(8,128)S(1)} custom-call(f32[193,128]{1,0:T(8,128)S(1)} %get-tuple-element.32.refs_0_, f32[193,128]{1,0:T(8,128)S(1)} %collective-permute-done.7.refs_1_, f32[193,128]{1,0:T(8,128)S(1)} %collective-permute-done.8.refs_2_), custom_call_target="tpu_custom_call" | custom-call | tf_op jit(solution)/shard_map/pallas_call | solution.py:166
  26.3 0.7 %collective-permute-done.6.refs_0_ = f32[193,128]{1,0:T(8,128)S(1)} collective-permute-done((f32[193,128]{1,0:T(8,128)S(1)}, f32[193,128]{1,0:T(8,128)S(1)}, u32[]{:S(2)}, u32[]{:S(2)}) %collective-permute-start.6) | collective-permute-done | bytes 98848 | tf_op jit(solution)/shard_map/ppermute | solution.py:225
  27.0 1.4 %shard_map.64 = f32[16,3072]{1,0:T(8,128)} custom-call(f32[193,128]{1,0:T(8,128)S(1)} %collective-permute-done.6.refs_0_, f32[16,3072]{1,0:T(8,128)S(1)} %shard_map.63.refs_1_), custom_call_target="tpu_custom_call" | custom-call | tf_op jit(solution)/shard_map/pallas_call | solution.py:166
  (9 shorter events, 0.2 us)
Async XLA Ops:
  0.0 0.7 %copy-start.1 = (s32[64,2]{0,1:T(2,128)S(1)}, s32[64,2]{0,1:T(2,128)}, u32[]{:S(2)}) copy-start(s32[64,2]{0,1:T(2,128)} %param.7) | copy-start | bytes 1540
  0.0 0.7 %copy-start.2 = (s32[256]{0:T(256)S(1)}, s32[256]{0:T(256)}, u32[]{:S(2)}) copy-start(s32[256]{0:T(256)} %param.9) | copy-start | bytes 3076
  0.0 0.9 %copy-start = (bf16[4096,16]{0,1:T(8,128)(2,1)S(1)}, bf16[4096,16]{0,1:T(8,128)(2,1)}, u32[]{:S(2)}) copy-start(bf16[4096,16]{0,1:T(8,128)(2,1)} %param.6) | copy-start | bytes 393220
  0.1 8.1 %copy-start.3 = (s32[24]{0:T(128)S(1)}, s32[24]{0:T(128)}, u32[]{:S(2)}) copy-start(s32[24]{0:T(128)} %param.8) | copy-start | bytes 292
  7.2 1.6 %collective-permute-start.2 = (f32[32,1536]{1,0:T(8,128)S(1)}, f32[32,1536]{1,0:T(8,128)S(1)}, u32[]{:S(2)}, u32[]{:S(2)}) collective-permute-start(f32[32,1536]{1,0:T(8,128)S(1)} %get-tuple-element.24), channel_id=1, source_target_pairs={{0,1},{1,0},{2,3},{3,2},{4,5},{5,4},{6,7},{7,6},{8,9},{9,8},{10,11... | collective-permute-start | bytes 589832 | tf_op jit(solution)/shard_map/ppermute | solution.py:225
  7.7 4.9 %collective-permute-start = (f32[64,1536]{1,0:T(8,128)S(1)}, f32[64,1536]{1,0:T(8,128)S(1)}, u32[]{:S(2)}, u32[]{:S(2)}) collective-permute-start(f32[64,1536]{1,0:T(8,128)S(1)} %get-tuple-element.20), channel_id=1, source_target_pairs={{0,1},{1,0},{2,3},{3,2},{4,5},{5,4},{6,7},{7,6},{8,9},{9,8},{10,11... | collective-permute-start | bytes 1179656 | tf_op jit(solution)/shard_map/ppermute | solution.py:225
  7.7 4.0 %collective-permute-start.1 = (f32[32,1536]{1,0:T(8,128)S(1)}, f32[32,1536]{1,0:T(8,128)S(1)}, u32[]{:S(2)}, u32[]{:S(2)}) collective-permute-start(f32[32,1536]{1,0:T(8,128)S(1)} %get-tuple-element.22), channel_id=1, source_target_pairs={{0,1},{1,0},{2,3},{3,2},{4,5},{5,4},{6,7},{7,6},{8,9},{9,8},{10,11... | collective-permute-start | bytes 589832 | tf_op jit(solution)/shard_map/ppermute | solution.py:225
  8.8 6.5 %collective-permute-start.5 = (f32[16,1536]{1,0:T(8,128)S(1)}, f32[16,1536]{1,0:T(8,128)S(1)}, u32[]{:S(2)}, u32[]{:S(2)}) collective-permute-start(f32[16,1536]{1,0:T(8,128)S(1)} %get-tuple-element.30), channel_id=1, source_target_pairs={{0,2},{1,3},{2,0},{3,1},{4,6},{5,7},{6,4},{7,5},{8,10},{9,11},{10,... | collective-permute-start | bytes 294920 | tf_op jit(solution)/shard_map/ppermute | solution.py:225
  11.7 6.8 %collective-permute-start.4 = (f32[16,1536]{1,0:T(8,128)S(1)}, f32[16,1536]{1,0:T(8,128)S(1)}, u32[]{:S(2)}, u32[]{:S(2)}) collective-permute-start(f32[16,1536]{1,0:T(8,128)S(1)} %get-tuple-element.29), channel_id=1, source_target_pairs={{0,2},{1,3},{2,0},{3,1},{4,6},{5,7},{6,4},{7,5},{8,10},{9,11},{10,... | collective-permute-start | bytes 294920 | tf_op jit(solution)/shard_map/ppermute | solution.py:225
  12.6 9.0 %collective-permute-start.3 = (f32[32,1536]{1,0:T(8,128)S(1)}, f32[32,1536]{1,0:T(8,128)S(1)}, u32[]{:S(2)}, u32[]{:S(2)}) collective-permute-start(f32[32,1536]{1,0:T(8,128)S(1)} %get-tuple-element.28), channel_id=1, source_target_pairs={{0,2},{1,3},{2,0},{3,1},{4,6},{5,7},{6,4},{7,5},{8,10},{9,11},{10,... | collective-permute-start | bytes 589832 | tf_op jit(solution)/shard_map/ppermute | solution.py:225
  15.3 10.1 %collective-permute-start.7 = (f32[193,128]{1,0:T(8,128)S(1)}, f32[193,128]{1,0:T(8,128)S(1)}, u32[]{:S(2)}, u32[]{:S(2)}) collective-permute-start(f32[193,128]{1,0:T(8,128)S(1)} %shard_map.60.earlier), channel_id=1, source_target_pairs={{0,8},{4,12},{8,0},{12,4},{1,9},{5,13},{9,1},{13,5},{2,10},{6,14},... | collective-permute-start | bytes 296456 | tf_op jit(solution)/shard_map/ppermute | solution.py:225
  18.5 6.7 %collective-permute-start.8 = (f32[193,128]{1,0:T(8,128)S(1)}, f32[193,128]{1,0:T(8,128)S(1)}, u32[]{:S(2)}, u32[]{:S(2)}) collective-permute-start(f32[193,128]{1,0:T(8,128)S(1)} %shard_map.61.earlier), channel_id=1, source_target_pairs={{0,12},{4,8},{8,4},{12,0},{1,13},{5,9},{9,5},{13,1},{2,14},{6,10},... | collective-permute-start | bytes 296456 | tf_op jit(solution)/shard_map/ppermute | solution.py:225
  21.7 5.4 %collective-permute-start.6 = (f32[193,128]{1,0:T(8,128)S(1)}, f32[193,128]{1,0:T(8,128)S(1)}, u32[]{:S(2)}, u32[]{:S(2)}) collective-permute-start(f32[193,128]{1,0:T(8,128)S(1)} %get-tuple-element.31), channel_id=1, source_target_pairs={{0,4},{4,0},{8,12},{12,8},{1,5},{5,1},{9,13},{13,9},{2,6},{6,2},{1... | collective-permute-start | bytes 296456 | tf_op jit(solution)/shard_map/ppermute | solution.py:225

commit v6 on v5

--- a/solution.py
+++ b/solution.py
@@ -135,23 +135,19 @@
 
 
 def place_kernel(slots, count, *refs):
-    pieces, before = refs[:count], refs[count:-4]
-    out, numbers, scalars, sem = refs[-4:]
+    pieces, before = refs[:count], refs[count:-1]
+    out = refs[-1]
     rows = out.shape[0]
-    for d, piece in enumerate(pieces):
-        numbers[pl.ds(d, 1), :] = piece[pl.ds(slots // 2 * rows, 1), :].astype(jnp.int32)
-    copy = pltpu.make_async_copy(numbers, scalars, sem)
-    copy.start()
     for done in before:
         out[...] = done[...]
-    copy.wait()
     upper = lax.broadcasted_iota(jnp.int32, (out.shape[0], LANES), 1) // BLOCK_PAIRS
-    for d, piece in enumerate(pieces):
+    for piece in pieces:
+        ids = piece[pl.ds(slots // 2 * rows, 1), :].astype(jnp.int32)
         for tile in range(slots // 2):
             value = piece[pl.ds(tile * rows, rows), :]
             turned = pltpu.roll(value, BLOCK_PAIRS, 1)
             for side in range(2):
-                block = scalars[d, 2 * tile + side]
+                block = ids[0, 2 * tile + side]
                 there = (jnp.maximum(block, 0) >> 1) * LANES
                 pltpu.store(
                     out.at[:, pl.ds(pl.multiple_of(there, LANES), LANES)],
@@ -168,11 +164,6 @@
         out_shape=jax.ShapeDtypeStruct((rows, blocks * BLOCK_PAIRS), jnp.float32),
         in_specs=[vmem] * (len(pieces) + len(before)),
         out_specs=vmem,
-        scratch_shapes=[
-            pltpu.VMEM((len(pieces), LANES), jnp.int32),
-            pltpu.SMEM((len(pieces), LANES), jnp.int32),
-            pltpu.SemaphoreType.DMA,
-        ],
         compiler_params=pltpu.CompilerParams(vmem_limit_bytes=8 * MIB),
     )(*pieces, *before)
 

time: 28.5 us -> 28 us (0.982)
  Pallas kernels: 8.6 us -> 7.66 us
  waiting for transfers between devices: 5.01 us -> 5.47 us
    pallas_call x2, Pallas kernels: 2.21 us -> 1.27 us  [placed_rows(): pl.pallas_call(functools.partial(place_kernel, slots, len(pieces)), out_s...]
    ppermute x9, waiting for transfers between devices: 5.01 us -> 5.47 us  [swap(): return lax.ppermute(value, axis, [(i, i ^ far) for i in range(size)])]
  transfers between devices with their start and end apart: 9 -> 9, of which waited for: 5 -> 5; matrix products, arithmetic and copies ran while one was open for 0% -> 0% of each run, Pallas kernels for 4% -> 2%
where the time goes in v6:
time: 28 us; the launch traced here: 27.9 us
  starting transfers between devices  13.8 us (49%)
  Pallas kernels  7.66 us (27%)
  waiting for transfers between devices  5.47 us (20%)
  local copies, waits for them, and re-layouts  0.88 us (3%)
    ppermute x9, starting transfers between devices, swap(): return lax.ppermute(value, axis, [(i, i ^ far) for i in range(size)])  13.8 us
    pallas_call x1, Pallas kernels, half_rows(): pl.pallas_call(functools.partial(half_rows_kernel, spans), out_shape=part...  6.21 us
    ppermute x9, waiting for transfers between devices, swap(): return lax.ppermute(value, axis, [(i, i ^ far) for i in range(size)])  5.47 us
    pallas_call x2, Pallas kernels, placed_rows(): pl.pallas_call(functools.partial(place_kernel, slots, len(pieces)), out_s...  1.27 us
    unnamed x8, local copies, waits for them, and re-layouts  0.88 us
  transfers between devices with their start and end apart: 9, of which 5 were waited for; matrix products, arithmetic and copies ran while one was open for 0% of the time, Pallas kernels for 2%

profile of v6, /device:TPU:0, one launch (start us, length us, event | category | flops | bytes accessed | tf_op | source)
XLA Modules:
  0.0 27.9 jit_solution(10476513758437359452)
XLA Ops:
  0.0 0.0 copy-start.1
  0.0 0.0 copy-start.2
  0.0 0.0 copy-start
  0.1 0.0 copy-start.3
  0.1 0.6 %copy-done.1 = s32[64,2]{0,1:T(2,128)S(1)} copy-done((s32[64,2]{0,1:T(2,128)S(1)}, s32[64,2]{0,1:T(2,128)}, u32[]{:S(2)}) %copy-start.1) | copy-done | bytes 536
  0.7 0.0 copy-done.2
  0.7 0.2 copy-done
  0.9 6.2 %shard_map.56 = (f32[64,1536]{1,0:T(8,128)S(1)}, f32[32,1536]{1,0:T(8,128)S(1)}, f32[32,1536]{1,0:T(8,128)S(1)}, f32[64,1536]{1,0:T(8,128)S(1)}, f32[32,1536]{1,0:T(8,128)S(1)}, /*index=5*/f32[32,1536]{1,0:T(8,128)S(1)}) custom-call(s32[2,64]{1,0:T(2,128)S(1)} %bitcast.6, s32[1,256]{1,0:T(1,128)S(1)} %bitcast.7, bf16[16,4096]{1,0:T(8,128)(2,1)S(1)} %bitcast.5, ...), custom_call_target="tpu_custom_call" | custom-call | tf_op jit(solution)/shard_map/pallas_call | solution.py:118
  7.2 0.5 %collective-permute-start.2 = (f32[32,1536]{1,0:T(8,128)S(1)}, f32[32,1536]{1,0:T(8,128)S(1)}, u32[]{:S(2)}, u32[]{:S(2)}) collective-permute-start(f32[32,1536]{1,0:T(8,128)S(1)} %get-tuple-element.24), channel_id=1, source_target_pairs={{0,1},{1,0},{2,3},{3,2},{4,5},{5,4},{6,7},{7,6},{8,9},{9,8},{10,11... | collective-permute-start | bytes 589832 | tf_op jit(solution)/shard_map/ppermute | solution.py:216
  7.7 0.1 collective-permute-start
  7.7 0.4 %collective-permute-start.1 = (f32[32,1536]{1,0:T(8,128)S(1)}, f32[32,1536]{1,0:T(8,128)S(1)}, u32[]{:S(2)}, u32[]{:S(2)}) collective-permute-start(f32[32,1536]{1,0:T(8,128)S(1)} %get-tuple-element.22), channel_id=1, source_target_pairs={{0,1},{1,0},{2,3},{3,2},{4,5},{5,4},{6,7},{7,6},{8,9},{9,8},{10,11... | collective-permute-start | bytes 589832 | tf_op jit(solution)/shard_map/ppermute | solution.py:216
  8.2 0.0 copy-done.3
  8.2 0.6 %collective-permute-done.2.theirs.earlier = f32[32,1536]{1,0:T(8,128)S(1)} collective-permute-done((f32[32,1536]{1,0:T(8,128)S(1)}, f32[32,1536]{1,0:T(8,128)S(1)}, u32[]{:S(2)}, u32[]{:S(2)}) %collective-permute-start.2) | collective-permute-done | bytes 196640 | tf_op jit(solution)/shard_map/ppermute | solution.py:216
  8.8 2.9 %collective-permute-start.5 = (f32[16,1536]{1,0:T(8,128)S(1)}, f32[16,1536]{1,0:T(8,128)S(1)}, u32[]{:S(2)}, u32[]{:S(2)}) collective-permute-start(f32[16,1536]{1,0:T(8,128)S(1)} %get-tuple-element.30), channel_id=1, source_target_pairs={{0,2},{1,3},{2,0},{3,1},{4,6},{5,7},{6,4},{7,5},{8,10},{9,11},{10,... | collective-permute-start | bytes 294920 | tf_op jit(solution)/shard_map/ppermute | solution.py:216
  11.7 0.0 collective-permute-done.1.theirs
  11.7 0.8 %collective-permute-start.4 = (f32[16,1536]{1,0:T(8,128)S(1)}, f32[16,1536]{1,0:T(8,128)S(1)}, u32[]{:S(2)}, u32[]{:S(2)}) collective-permute-start(f32[16,1536]{1,0:T(8,128)S(1)} %get-tuple-element.29), channel_id=1, source_target_pairs={{0,2},{1,3},{2,0},{3,1},{4,6},{5,7},{6,4},{7,5},{8,10},{9,11},{10,... | collective-permute-start | bytes 294920 | tf_op jit(solution)/shard_map/ppermute | solution.py:216
  12.5 0.0 collective-permute-done.theirs
  12.6 1.3 %collective-permute-start.3 = (f32[32,1536]{1,0:T(8,128)S(1)}, f32[32,1536]{1,0:T(8,128)S(1)}, u32[]{:S(2)}, u32[]{:S(2)}) collective-permute-start(f32[32,1536]{1,0:T(8,128)S(1)} %get-tuple-element.28), channel_id=1, source_target_pairs={{0,2},{1,3},{2,0},{3,1},{4,6},{5,7},{6,4},{7,5},{8,10},{9,11},{10,... | collective-permute-start | bytes 589832 | tf_op jit(solution)/shard_map/ppermute | solution.py:216
  13.9 1.3 %collective-permute-done.5.theirs = f32[16,1536]{1,0:T(8,128)S(1)} collective-permute-done((f32[16,1536]{1,0:T(8,128)S(1)}, f32[16,1536]{1,0:T(8,128)S(1)}, u32[]{:S(2)}, u32[]{:S(2)}) %collective-permute-start.5) | collective-permute-done | bytes 98336 | tf_op jit(solution)/shard_map/ppermute | solution.py:216
  15.3 3.2 %collective-permute-start.7 = (f32[193,128]{1,0:T(8,128)S(1)}, f32[193,128]{1,0:T(8,128)S(1)}, u32[]{:S(2)}, u32[]{:S(2)}) collective-permute-start(f32[193,128]{1,0:T(8,128)S(1)} %shard_map.60.earlier), channel_id=1, source_target_pairs={{0,8},{4,12},{8,0},{12,4},{1,9},{5,13},{9,1},{13,5},{2,10},{6,14},... | collective-permute-start | bytes 296456 | tf_op jit(solution)/shard_map/ppermute | solution.py:216
  18.5 0.0 collective-permute-done.4.theirs
  18.5 3.1 %collective-permute-start.8 = (f32[193,128]{1,0:T(8,128)S(1)}, f32[193,128]{1,0:T(8,128)S(1)}, u32[]{:S(2)}, u32[]{:S(2)}) collective-permute-start(f32[193,128]{1,0:T(8,128)S(1)} %shard_map.61.earlier), channel_id=1, source_target_pairs={{0,12},{4,8},{8,4},{12,0},{1,13},{5,9},{9,5},{13,1},{2,14},{6,10},... | collective-permute-start | bytes 296456 | tf_op jit(solution)/shard_map/ppermute | solution.py:216
  21.6 0.0 collective-permute-done.3.theirs
  21.7 1.4 %collective-permute-start.6 = (f32[193,128]{1,0:T(8,128)S(1)}, f32[193,128]{1,0:T(8,128)S(1)}, u32[]{:S(2)}, u32[]{:S(2)}) collective-permute-start(f32[193,128]{1,0:T(8,128)S(1)} %get-tuple-element.31), channel_id=1, source_target_pairs={{0,4},{4,0},{8,12},{12,8},{1,5},{5,1},{9,13},{13,9},{2,6},{6,2},{1... | collective-permute-start | bytes 296456 | tf_op jit(solution)/shard_map/ppermute | solution.py:216
  23.0 2.2 %collective-permute-done.8.refs_2_ = f32[193,128]{1,0:T(8,128)S(1)} collective-permute-done((f32[193,128]{1,0:T(8,128)S(1)}, f32[193,128]{1,0:T(8,128)S(1)}, u32[]{:S(2)}, u32[]{:S(2)}) %collective-permute-start.8) | collective-permute-done | bytes 98848 | tf_op jit(solution)/shard_map/ppermute | solution.py:216
  25.2 0.2 collective-permute-done.7.refs_1_
  25.4 0.4 %shard_map.63.refs_1_ = f32[16,3072]{1,0:T(8,128)S(1)} custom-call(f32[193,128]{1,0:T(8,128)S(1)} %get-tuple-element.32.refs_0_, f32[193,128]{1,0:T(8,128)S(1)} %collective-permute-done.7.refs_1_, f32[193,128]{1,0:T(8,128)S(1)} %collective-permute-done.8.refs_2_), custom_call_target="tpu_custom_call" | custom-call | tf_op jit(solution)/shard_map/pallas_call | solution.py:162
  25.8 1.2 %collective-permute-done.6.refs_0_ = f32[193,128]{1,0:T(8,128)S(1)} collective-permute-done((f32[193,128]{1,0:T(8,128)S(1)}, f32[193,128]{1,0:T(8,128)S(1)}, u32[]{:S(2)}, u32[]{:S(2)}) %collective-permute-start.6) | collective-permute-done | bytes 98848 | tf_op jit(solution)/shard_map/ppermute | solution.py:216
  27.0 0.9 %shard_map.64 = f32[16,3072]{1,0:T(8,128)} custom-call(f32[193,128]{1,0:T(8,128)S(1)} %collective-permute-done.6.refs_0_, f32[16,3072]{1,0:T(8,128)S(1)} %shard_map.63.refs_1_), custom_call_target="tpu_custom_call" | custom-call | tf_op jit(solution)/shard_map/pallas_call | solution.py:162
  (9 shorter events, 0.2 us)
Async XLA Ops:
  0.0 0.7 %copy-start.1 = (s32[64,2]{0,1:T(2,128)S(1)}, s32[64,2]{0,1:T(2,128)}, u32[]{:S(2)}) copy-start(s32[64,2]{0,1:T(2,128)} %param.7) | copy-start | bytes 1540
  0.0 0.7 %copy-start.2 = (s32[256]{0:T(256)S(1)}, s32[256]{0:T(256)}, u32[]{:S(2)}) copy-start(s32[256]{0:T(256)} %param.9) | copy-start | bytes 3076
  0.0 0.9 %copy-start = (bf16[4096,16]{0,1:T(8,128)(2,1)S(1)}, bf16[4096,16]{0,1:T(8,128)(2,1)}, u32[]{:S(2)}) copy-start(bf16[4096,16]{0,1:T(8,128)(2,1)} %param.6) | copy-start | bytes 393220
  0.1 8.1 %copy-start.3 = (s32[24]{0:T(128)S(1)}, s32[24]{0:T(128)}, u32[]{:S(2)}) copy-start(s32[24]{0:T(128)} %param.8) | copy-start | bytes 292
  7.2 1.6 %collective-permute-start.2 = (f32[32,1536]{1,0:T(8,128)S(1)}, f32[32,1536]{1,0:T(8,128)S(1)}, u32[]{:S(2)}, u32[]{:S(2)}) collective-permute-start(f32[32,1536]{1,0:T(8,128)S(1)} %get-tuple-element.24), channel_id=1, source_target_pairs={{0,1},{1,0},{2,3},{3,2},{4,5},{5,4},{6,7},{7,6},{8,9},{9,8},{10,11... | collective-permute-start | bytes 589832 | tf_op jit(solution)/shard_map/ppermute | solution.py:216
  7.7 4.9 %collective-permute-start = (f32[64,1536]{1,0:T(8,128)S(1)}, f32[64,1536]{1,0:T(8,128)S(1)}, u32[]{:S(2)}, u32[]{:S(2)}) collective-permute-start(f32[64,1536]{1,0:T(8,128)S(1)} %get-tuple-element.20), channel_id=1, source_target_pairs={{0,1},{1,0},{2,3},{3,2},{4,5},{5,4},{6,7},{7,6},{8,9},{9,8},{10,11... | collective-permute-start | bytes 1179656 | tf_op jit(solution)/shard_map/ppermute | solution.py:216
  7.7 4.0 %collective-permute-start.1 = (f32[32,1536]{1,0:T(8,128)S(1)}, f32[32,1536]{1,0:T(8,128)S(1)}, u32[]{:S(2)}, u32[]{:S(2)}) collective-permute-start(f32[32,1536]{1,0:T(8,128)S(1)} %get-tuple-element.22), channel_id=1, source_target_pairs={{0,1},{1,0},{2,3},{3,2},{4,5},{5,4},{6,7},{7,6},{8,9},{9,8},{10,11... | collective-permute-start | bytes 589832 | tf_op jit(solution)/shard_map/ppermute | solution.py:216
  8.8 6.5 %collective-permute-start.5 = (f32[16,1536]{1,0:T(8,128)S(1)}, f32[16,1536]{1,0:T(8,128)S(1)}, u32[]{:S(2)}, u32[]{:S(2)}) collective-permute-start(f32[16,1536]{1,0:T(8,128)S(1)} %get-tuple-element.30), channel_id=1, source_target_pairs={{0,2},{1,3},{2,0},{3,1},{4,6},{5,7},{6,4},{7,5},{8,10},{9,11},{10,... | collective-permute-start | bytes 294920 | tf_op jit(solution)/shard_map/ppermute | solution.py:216
  11.7 6.8 %collective-permute-start.4 = (f32[16,1536]{1,0:T(8,128)S(1)}, f32[16,1536]{1,0:T(8,128)S(1)}, u32[]{:S(2)}, u32[]{:S(2)}) collective-permute-start(f32[16,1536]{1,0:T(8,128)S(1)} %get-tuple-element.29), channel_id=1, source_target_pairs={{0,2},{1,3},{2,0},{3,1},{4,6},{5,7},{6,4},{7,5},{8,10},{9,11},{10,... | collective-permute-start | bytes 294920 | tf_op jit(solution)/shard_map/ppermute | solution.py:216
  12.6 9.0 %collective-permute-start.3 = (f32[32,1536]{1,0:T(8,128)S(1)}, f32[32,1536]{1,0:T(8,128)S(1)}, u32[]{:S(2)}, u32[]{:S(2)}) collective-permute-start(f32[32,1536]{1,0:T(8,128)S(1)} %get-tuple-element.28), channel_id=1, source_target_pairs={{0,2},{1,3},{2,0},{3,1},{4,6},{5,7},{6,4},{7,5},{8,10},{9,11},{10,... | collective-permute-start | bytes 589832 | tf_op jit(solution)/shard_map/ppermute | solution.py:216
  15.3 10.1 %collective-permute-start.7 = (f32[193,128]{1,0:T(8,128)S(1)}, f32[193,128]{1,0:T(8,128)S(1)}, u32[]{:S(2)}, u32[]{:S(2)}) collective-permute-start(f32[193,128]{1,0:T(8,128)S(1)} %shard_map.60.earlier), channel_id=1, source_target_pairs={{0,8},{4,12},{8,0},{12,4},{1,9},{5,13},{9,1},{13,5},{2,10},{6,14},... | collective-permute-start | bytes 296456 | tf_op jit(solution)/shard_map/ppermute | solution.py:216
  18.5 6.7 %collective-permute-start.8 = (f32[193,128]{1,0:T(8,128)S(1)}, f32[193,128]{1,0:T(8,128)S(1)}, u32[]{:S(2)}, u32[]{:S(2)}) collective-permute-start(f32[193,128]{1,0:T(8,128)S(1)} %shard_map.61.earlier), channel_id=1, source_target_pairs={{0,12},{4,8},{8,4},{12,0},{1,13},{5,9},{9,5},{13,1},{2,14},{6,10},... | collective-permute-start | bytes 296456 | tf_op jit(solution)/shard_map/ppermute | solution.py:216
  21.7 5.4 %collective-permute-start.6 = (f32[193,128]{1,0:T(8,128)S(1)}, f32[193,128]{1,0:T(8,128)S(1)}, u32[]{:S(2)}, u32[]{:S(2)}) collective-permute-start(f32[193,128]{1,0:T(8,128)S(1)} %get-tuple-element.31), channel_id=1, source_target_pairs={{0,4},{4,0},{8,12},{12,8},{1,5},{5,1},{9,13},{13,9},{2,6},{6,2},{1... | collective-permute-start | bytes 296456 | tf_op jit(solution)/shard_map/ppermute | solution.py:216

commit v7 on v6

--- a/solution.py
+++ b/solution.py
@@ -25,17 +25,14 @@
     place = lax.broadcasted_iota(jnp.int32, (SHELL, NIJ), 1)
     inner = place % rows_each
     block = place // rows_each
-    step, some, chips = pairs // 2, max(pairs // 4, 1), ranges // 2
+    some, chips = max(pairs // 4, 1), ranges // 2
     core = block // (pairs * chips)
-    high = (block // (step * chips)) % 2
-    block = block % (step * chips)
-    far = high == 1
-    low = jnp.where(far, (block // (some * chips)) * some + block % some, block % step)
-    order = jnp.where(far, (block // some) % chips, block // step)
+    block = block % (pairs * chips)
+    order = (block // some) % chips
     far_range = core
     for bit in range(1, bits(ranges)):
         far_range = far_range + (((order >> (bits(ranges) - 1 - bit)) & 1) << bit)
-    far_pair = low + high * step
+    far_pair = (block // (some * chips)) * some + block % some
     target = ((far_pair ^ me_pair) * ranges + (far_range ^ me_range)) * rows_each + inner
     row = lax.broadcasted_iota(jnp.int32, (NIJ, NIJ), 0)
     moved[...] = (row == target[0:1, :]).astype(jnp.bfloat16)
@@ -219,42 +216,40 @@
 def local(pairs, ranges, integrals, coefficients, ket_shells, block_ids, pair_owner):
     slots = block_ids.shape[0]
     each = NIJ // (pairs * ranges)
-    step = pairs // 2
-    some = max(step // 2, 1)
-    groups = [(0, step)] + [(step + at, some) for at in range(0, step, some)]
-    sizes = [count * each * (ranges // 2) for _, count in groups]
+    some = max(pairs // 4, 1)
+    firsts = list(range(0, pairs, some))
+    sizes = [some * each * (ranges // 2) for _ in firsts]
     parts = half_rows(integrals, coefficients, ket_shells, pair_owner, pairs, ranges, sizes)
     numbers = jnp.pad(block_ids.astype(jnp.float32), (0, LANES - slots)).reshape(1, LANES)
-    groups = [
-        (first, count, parts[at], parts[at + len(groups)])
-        for at, (first, count) in enumerate(groups)
-    ]
-    groups = [
-        (first, count, mine, swap(send, "rng", ranges, 1))
-        for first, count, mine, send in groups[1:] + groups[:1]
-    ]
+    step = pairs // 2
+    firsts = firsts[step // some :: -1] + firsts[step // some + 1 :]
+    firsts = firsts[:2] + firsts[3:] + firsts[2:3]
+    groups = []
+    for first in firsts:
+        at = first // some
+        groups.append((first, parts[at], swap(parts[at + len(sizes)], "rng", ranges, 1)))
     halves = []
-    earlier = groups[0][3]
-    for first, count, mine, theirs in groups:
-        lower, upper = summed(mine, theirs, earlier, 5 * 10**8)
-        halves.append((first, count, lower, upper))
+    earlier = groups[0][2]
+    for first, mine, theirs in groups:
+        lower, upper = summed(mine, theirs, earlier, 10**6)
+        halves.append((first, lower, upper))
         earlier = lower
     pieces = [None] * pairs
     earlier = numbers
-    for first, count, lower, upper in halves:
+    for first, lower, upper in halves:
         for bit in range(1, bits(ranges)):
             other = swap(upper, "rng", ranges, 1 << bit)
             if bit < bits(ranges) - 1:
                 lower = lower + other
                 lower, upper = jnp.split(lower, 2)
-        parts = merged(lower, other, numbers, earlier, count, 10**9 if first == step else 2 * 10**9)
+        parts = merged(lower, other, numbers, earlier, some, 2 * 10**9 if first == pairs - some else 5 * 10**8)
         earlier = parts[0]
-        for at in range(count):
+        for at in range(some):
             d = first + at
             pieces[d] = swap(parts[at], "pair", pairs, d) if d else parts[at]
     blocks = slots * pairs // 2
-    early = placed_rows(pieces[:1] + pieces[step:], [], slots, blocks)
-    return placed_rows(pieces[1:step], [early], slots, blocks) if step > 1 else early
+    early = placed_rows(pieces[:-some], [], slots, blocks)
+    return placed_rows(pieces[-some:], [early], slots, blocks)
 
 
 def solution(mesh):

time: 28 us -> 27.8 us (level)
  waiting for transfers between devices: 5.47 us -> 4.16 us
  starting transfers between devices: 13.8 us -> 14.8 us
    ppermute x9 -> x11, waiting for transfers between devices: 5.47 us -> 4.16 us  [swap(): return lax.ppermute(value, axis, [(i, i ^ far) for i in range(size)])]
    ppermute x9 -> x11, starting transfers between devices: 13.8 us -> 14.8 us  [swap(): return lax.ppermute(value, axis, [(i, i ^ far) for i in range(size)])]
  transfers between devices with their start and end apart: 9 -> 11, of which waited for: 5 -> 3; matrix products, arithmetic and copies ran while one was open for 0% -> 0% of each run, Pallas kernels for 2% -> 2%
where the time goes in v7:
time: 27.8 us; the launch traced here: 27.6 us
  starting transfers between devices  14.8 us (53%)
  Pallas kernels  7.66 us (28%)
  waiting for transfers between devices  4.16 us (15%)
  local copies, waits for them, and re-layouts  0.88 us (3%)
    ppermute x11, starting transfers between devices, swap(): return lax.ppermute(value, axis, [(i, i ^ far) for i in range(size)])  14.8 us
    pallas_call x1, Pallas kernels, half_rows(): pl.pallas_call(functools.partial(half_rows_kernel, spans), out_shape=part...  6.21 us
    ppermute x11, waiting for transfers between devices, swap(): return lax.ppermute(value, axis, [(i, i ^ far) for i in range(size)])  4.16 us
    pallas_call x2, Pallas kernels, placed_rows(): pl.pallas_call(functools.partial(place_kernel, slots, len(pieces)), out_s...  1.27 us
    unnamed x8, local copies, waits for them, and re-layouts  0.88 us
  transfers between devices with their start and end apart: 11, of which 3 were waited for; matrix products, arithmetic and copies ran while one was open for 0% of the time, Pallas kernels for 2%

profile of v7, /device:TPU:0, one launch (start us, length us, event | category | flops | bytes accessed | tf_op | source)
XLA Modules:
  0.0 27.6 jit_solution(5579392495778540828)
XLA Ops:
  0.0 0.0 copy-start.1
  0.0 0.0 copy-start.2
  0.0 0.0 copy-start
  0.1 0.0 copy-start.3
  0.1 0.6 %copy-done.1 = s32[64,2]{0,1:T(2,128)S(1)} copy-done((s32[64,2]{0,1:T(2,128)S(1)}, s32[64,2]{0,1:T(2,128)}, u32[]{:S(2)}) %copy-start.1) | copy-done | bytes 536
  0.7 0.0 copy-done.2
  0.7 0.2 copy-done
  0.9 6.2 %shard_map.56 = (f32[32,1536]{1,0:T(8,128)S(1)}, f32[32,1536]{1,0:T(8,128)S(1)}, f32[32,1536]{1,0:T(8,128)S(1)}, f32[32,1536]{1,0:T(8,128)S(1)}, f32[32,1536]{1,...) custom-call(s32[2,64]{1,0:T(2,128)S(1)} %bitcast.6, s32[1,256]{1,0:T(1,128)S(1)} %bitcast.7, ...), custom_call_target="tpu_custom_call" | custom-call | tf_op jit(solution)/shard_map/pallas_call | solution.py:115
  7.2 0.5 %collective-permute-start.2 = (f32[32,1536]{1,0:T(8,128)S(1)}, f32[32,1536]{1,0:T(8,128)S(1)}, u32[]{:S(2)}, u32[]{:S(2)}) collective-permute-start(f32[32,1536]{1,0:T(8,128)S(1)} %get-tuple-element.26), channel_id=1, source_target_pairs={{0,1},{1,0},{2,3},{3,2},{4,5},{5,4},{6,7},{7,6},{8,9},{9,8},{10,11... | collective-permute-start | bytes 589832 | tf_op jit(solution)/shard_map/ppermute | solution.py:213
  7.7 0.1 collective-permute-start.1
  7.7 0.4 %collective-permute-start = (f32[32,1536]{1,0:T(8,128)S(1)}, f32[32,1536]{1,0:T(8,128)S(1)}, u32[]{:S(2)}, u32[]{:S(2)}) collective-permute-start(f32[32,1536]{1,0:T(8,128)S(1)} %get-tuple-element.22), channel_id=1, source_target_pairs={{0,1},{1,0},{2,3},{3,2},{4,5},{5,4},{6,7},{7,6},{8,9},{9,8},{10,11... | collective-permute-start | bytes 589832 | tf_op jit(solution)/shard_map/ppermute | solution.py:213
  8.2 0.1 collective-permute-start.7
  8.3 0.0 copy-done.3
  8.3 0.5 %collective-permute-done.2.theirs.earlier = f32[32,1536]{1,0:T(8,128)S(1)} collective-permute-done((f32[32,1536]{1,0:T(8,128)S(1)}, f32[32,1536]{1,0:T(8,128)S(1)}, u32[]{:S(2)}, u32[]{:S(2)}) %collective-permute-start.2) | collective-permute-done | bytes 196640 | tf_op jit(solution)/shard_map/ppermute | solution.py:213
  8.8 2.9 %collective-permute-start.5 = (f32[16,1536]{1,0:T(8,128)S(1)}, f32[16,1536]{1,0:T(8,128)S(1)}, u32[]{:S(2)}, u32[]{:S(2)}) collective-permute-start(f32[16,1536]{1,0:T(8,128)S(1)} %get-tuple-element.32), channel_id=1, source_target_pairs={{0,2},{1,3},{2,0},{3,1},{4,6},{5,7},{6,4},{7,5},{8,10},{9,11},{10,... | collective-permute-start | bytes 294920 | tf_op jit(solution)/shard_map/ppermute | solution.py:213
  11.7 0.0 collective-permute-done.1.theirs
  11.7 0.3 collective-permute-start.4
  12.0 0.0 collective-permute-done.theirs
  12.0 1.9 %collective-permute-start.3 = (f32[16,1536]{1,0:T(8,128)S(1)}, f32[16,1536]{1,0:T(8,128)S(1)}, u32[]{:S(2)}, u32[]{:S(2)}) collective-permute-start(f32[16,1536]{1,0:T(8,128)S(1)} %get-tuple-element.30), channel_id=1, source_target_pairs={{0,2},{1,3},{2,0},{3,1},{4,6},{5,7},{6,4},{7,5},{8,10},{9,11},{10,... | collective-permute-start | bytes 294920 | tf_op jit(solution)/shard_map/ppermute | solution.py:213
  13.9 0.0 collective-permute-done.7.theirs
  13.9 0.3 collective-permute-start.8
  14.2 1.1 %collective-permute-done.5.theirs = f32[16,1536]{1,0:T(8,128)S(1)} collective-permute-done((f32[16,1536]{1,0:T(8,128)S(1)}, f32[16,1536]{1,0:T(8,128)S(1)}, u32[]{:S(2)}, u32[]{:S(2)}) %collective-permute-start.5) | collective-permute-done | bytes 98336 | tf_op jit(solution)/shard_map/ppermute | solution.py:213
  15.3 3.2 %collective-permute-start.10 = (f32[193,128]{1,0:T(8,128)S(1)}, f32[193,128]{1,0:T(8,128)S(1)}, u32[]{:S(2)}, u32[]{:S(2)}) collective-permute-start(f32[193,128]{1,0:T(8,128)S(1)} %shard_map.60.earlier), channel_id=1, source_target_pairs={{0,8},{4,12},{8,0},{12,4},{1,9},{5,13},{9,1},{13,5},{2,10},{6,14},... | collective-permute-start | bytes 296456 | tf_op jit(solution)/shard_map/ppermute | solution.py:213
  18.5 0.0 collective-permute-done.4.theirs
  18.5 1.6 %collective-permute-start.9 = (f32[193,128]{1,0:T(8,128)S(1)}, f32[193,128]{1,0:T(8,128)S(1)}, u32[]{:S(2)}, u32[]{:S(2)}) collective-permute-start(f32[193,128]{1,0:T(8,128)S(1)} %shard_map.61.earlier), channel_id=1, source_target_pairs={{0,4},{4,0},{8,12},{12,8},{1,5},{5,1},{9,13},{13,9},{2,6},{6,2},{1... | collective-permute-start | bytes 296456 | tf_op jit(solution)/shard_map/ppermute | solution.py:213
  20.2 0.0 collective-permute-done.3.theirs
  20.2 3.5 %collective-permute-start.6 = (f32[193,128]{1,0:T(8,128)S(1)}, f32[193,128]{1,0:T(8,128)S(1)}, u32[]{:S(2)}, u32[]{:S(2)}) collective-permute-start(f32[193,128]{1,0:T(8,128)S(1)} %shard_map.62.earlier), channel_id=1, source_target_pairs={{0,12},{4,8},{8,4},{12,0},{1,13},{5,9},{9,5},{13,1},{2,14},{6,10},... | collective-permute-start | bytes 296456 | tf_op jit(solution)/shard_map/ppermute | solution.py:213
  23.7 0.0 collective-permute-done.8.theirs
  23.7 0.0 collective-permute-done.9.refs_1_
  23.8 0.0 collective-permute-done.10.refs_2_
  23.8 0.4 %shard_map.65.refs_1_ = f32[16,3072]{1,0:T(8,128)S(1)} custom-call(f32[193,128]{1,0:T(8,128)S(1)} %shard_map.64.refs_0_, f32[193,128]{1,0:T(8,128)S(1)} %collective-permute-done.9.refs_1_, f32[193,128]{1,0:T(8,128)S(1)} %collective-permute-done.10.refs_2_), custom_call_target="tpu_custom_call" | custom-call | tf_op jit(solution)/shard_map/pallas_call | solution.py:159
  24.2 2.6 %collective-permute-done.6.refs_0_ = f32[193,128]{1,0:T(8,128)S(1)} collective-permute-done((f32[193,128]{1,0:T(8,128)S(1)}, f32[193,128]{1,0:T(8,128)S(1)}, u32[]{:S(2)}, u32[]{:S(2)}) %collective-permute-start.6) | collective-permute-done | bytes 98848 | tf_op jit(solution)/shard_map/ppermute | solution.py:213
  26.8 0.9 %shard_map.66 = f32[16,3072]{1,0:T(8,128)} custom-call(f32[193,128]{1,0:T(8,128)S(1)} %collective-permute-done.6.refs_0_, f32[16,3072]{1,0:T(8,128)S(1)} %shard_map.65.refs_1_), custom_call_target="tpu_custom_call" | custom-call | tf_op jit(solution)/shard_map/pallas_call | solution.py:159
  (11 shorter events, 0.2 us)
Async XLA Ops:
  0.0 0.7 %copy-start.1 = (s32[64,2]{0,1:T(2,128)S(1)}, s32[64,2]{0,1:T(2,128)}, u32[]{:S(2)}) copy-start(s32[64,2]{0,1:T(2,128)} %param.7) | copy-start | bytes 1540
  0.0 0.7 %copy-start.2 = (s32[256]{0:T(256)S(1)}, s32[256]{0:T(256)}, u32[]{:S(2)}) copy-start(s32[256]{0:T(256)} %param.9) | copy-start | bytes 3076
  0.0 0.9 %copy-start = (bf16[4096,16]{0,1:T(8,128)(2,1)S(1)}, bf16[4096,16]{0,1:T(8,128)(2,1)}, u32[]{:S(2)}) copy-start(bf16[4096,16]{0,1:T(8,128)(2,1)} %param.6) | copy-start | bytes 393220
  0.1 8.2 %copy-start.3 = (s32[24]{0:T(128)S(1)}, s32[24]{0:T(128)}, u32[]{:S(2)}) copy-start(s32[24]{0:T(128)} %param.8) | copy-start | bytes 292
  7.2 1.6 %collective-permute-start.2 = (f32[32,1536]{1,0:T(8,128)S(1)}, f32[32,1536]{1,0:T(8,128)S(1)}, u32[]{:S(2)}, u32[]{:S(2)}) collective-permute-start(f32[32,1536]{1,0:T(8,128)S(1)} %get-tuple-element.26), channel_id=1, source_target_pairs={{0,1},{1,0},{2,3},{3,2},{4,5},{5,4},{6,7},{7,6},{8,9},{9,8},{10,11... | collective-permute-start | bytes 589832 | tf_op jit(solution)/shard_map/ppermute | solution.py:213
  7.7 4.0 %collective-permute-start.1 = (f32[32,1536]{1,0:T(8,128)S(1)}, f32[32,1536]{1,0:T(8,128)S(1)}, u32[]{:S(2)}, u32[]{:S(2)}) collective-permute-start(f32[32,1536]{1,0:T(8,128)S(1)} %get-tuple-element.24), channel_id=1, source_target_pairs={{0,1},{1,0},{2,3},{3,2},{4,5},{5,4},{6,7},{7,6},{8,9},{9,8},{10,11... | collective-permute-start | bytes 589832 | tf_op jit(solution)/shard_map/ppermute | solution.py:213
  7.7 4.2 %collective-permute-start = (f32[32,1536]{1,0:T(8,128)S(1)}, f32[32,1536]{1,0:T(8,128)S(1)}, u32[]{:S(2)}, u32[]{:S(2)}) collective-permute-start(f32[32,1536]{1,0:T(8,128)S(1)} %get-tuple-element.22), channel_id=1, source_target_pairs={{0,1},{1,0},{2,3},{3,2},{4,5},{5,4},{6,7},{7,6},{8,9},{9,8},{10,11... | collective-permute-start | bytes 589832 | tf_op jit(solution)/shard_map/ppermute | solution.py:213
  8.2 5.7 %collective-permute-start.7 = (f32[32,1536]{1,0:T(8,128)S(1)}, f32[32,1536]{1,0:T(8,128)S(1)}, u32[]{:S(2)}, u32[]{:S(2)}) collective-permute-start(f32[32,1536]{1,0:T(8,128)S(1)} %get-tuple-element.34), channel_id=1, source_target_pairs={{0,1},{1,0},{2,3},{3,2},{4,5},{5,4},{6,7},{7,6},{8,9},{9,8},{10,11... | collective-permute-start | bytes 589832 | tf_op jit(solution)/shard_map/ppermute | solution.py:213
  8.8 6.5 %collective-permute-start.5 = (f32[16,1536]{1,0:T(8,128)S(1)}, f32[16,1536]{1,0:T(8,128)S(1)}, u32[]{:S(2)}, u32[]{:S(2)}) collective-permute-start(f32[16,1536]{1,0:T(8,128)S(1)} %get-tuple-element.32), channel_id=1, source_target_pairs={{0,2},{1,3},{2,0},{3,1},{4,6},{5,7},{6,4},{7,5},{8,10},{9,11},{10,... | collective-permute-start | bytes 294920 | tf_op jit(solution)/shard_map/ppermute | solution.py:213
  11.7 6.8 %collective-permute-start.4 = (f32[16,1536]{1,0:T(8,128)S(1)}, f32[16,1536]{1,0:T(8,128)S(1)}, u32[]{:S(2)}, u32[]{:S(2)}) collective-permute-start(f32[16,1536]{1,0:T(8,128)S(1)} %get-tuple-element.31), channel_id=1, source_target_pairs={{0,2},{1,3},{2,0},{3,1},{4,6},{5,7},{6,4},{7,5},{8,10},{9,11},{10,... | collective-permute-start | bytes 294920 | tf_op jit(solution)/shard_map/ppermute | solution.py:213
  12.0 8.2 %collective-permute-start.3 = (f32[16,1536]{1,0:T(8,128)S(1)}, f32[16,1536]{1,0:T(8,128)S(1)}, u32[]{:S(2)}, u32[]{:S(2)}) collective-permute-start(f32[16,1536]{1,0:T(8,128)S(1)} %get-tuple-element.30), channel_id=1, source_target_pairs={{0,2},{1,3},{2,0},{3,1},{4,6},{5,7},{6,4},{7,5},{8,10},{9,11},{10,... | collective-permute-start | bytes 294920 | tf_op jit(solution)/shard_map/ppermute | solution.py:213
  13.9 9.8 %collective-permute-start.8 = (f32[16,1536]{1,0:T(8,128)S(1)}, f32[16,1536]{1,0:T(8,128)S(1)}, u32[]{:S(2)}, u32[]{:S(2)}) collective-permute-start(f32[16,1536]{1,0:T(8,128)S(1)} %get-tuple-element.36), channel_id=1, source_target_pairs={{0,2},{1,3},{2,0},{3,1},{4,6},{5,7},{6,4},{7,5},{8,10},{9,11},{10,... | collective-permute-start | bytes 294920 | tf_op jit(solution)/shard_map/ppermute | solution.py:213
  15.3 8.5 %collective-permute-start.10 = (f32[193,128]{1,0:T(8,128)S(1)}, f32[193,128]{1,0:T(8,128)S(1)}, u32[]{:S(2)}, u32[]{:S(2)}) collective-permute-start(f32[193,128]{1,0:T(8,128)S(1)} %shard_map.60.earlier), channel_id=1, source_target_pairs={{0,8},{4,12},{8,0},{12,4},{1,9},{5,13},{9,1},{13,5},{2,10},{6,14},... | collective-permute-start | bytes 296456 | tf_op jit(solution)/shard_map/ppermute | solution.py:213
  18.5 5.2 %collective-permute-start.9 = (f32[193,128]{1,0:T(8,128)S(1)}, f32[193,128]{1,0:T(8,128)S(1)}, u32[]{:S(2)}, u32[]{:S(2)}) collective-permute-start(f32[193,128]{1,0:T(8,128)S(1)} %shard_map.61.earlier), channel_id=1, source_target_pairs={{0,4},{4,0},{8,12},{12,8},{1,5},{5,1},{9,13},{13,9},{2,6},{6,2},{1... | collective-permute-start | bytes 296456 | tf_op jit(solution)/shard_map/ppermute | solution.py:213
  20.2 6.6 %collective-permute-start.6 = (f32[193,128]{1,0:T(8,128)S(1)}, f32[193,128]{1,0:T(8,128)S(1)}, u32[]{:S(2)}, u32[]{:S(2)}) collective-permute-start(f32[193,128]{1,0:T(8,128)S(1)} %shard_map.62.earlier), channel_id=1, source_target_pairs={{0,12},{4,8},{8,4},{12,0},{1,13},{5,9},{9,5},{13,1},{2,14},{6,10},... | collective-permute-start | bytes 296456 | tf_op jit(solution)/shard_map/ppermute | solution.py:213
